TPU v7x, 32 devices: a whole 2x2x4 slice. The times are simulated.
32 devices in a mesh: sx: 4 (over y, x), sy: 8 (over z, core).
Axes of the slice: x: 2, y: 2, z: 4, core: 2. Of those that a mesh axis runs over, the one named last changes fastest.
Arguments:
- text_tokens: bfloat16 [8, 32, 4096], P('sy', 'sx'), may hold values from -2.5 to 2.5
- latent: bfloat16 [8, 16, 512], P('sy', 'sx'), may hold values from -6 to 6
- image_offset: int32 [8], P('sy'), may hold values from 0 to 32
- norm_gain: bfloat16 [4096], replicated, may hold values from 0.099609375 to 1.8984375
- w_query: bfloat16 [4096, 4096], P(None, 'sx')
- w_key: bfloat16 [4096, 4096], P(None, 'sx')
- w_value: bfloat16 [4096, 4096], P(None, 'sx'), may hold values from -0.09375 to 0.09375
- w_out: bfloat16 [4096, 4096], P('sx'), may hold values from -0.09375 to 0.09375
- w_down_conv: bfloat16 [288, 128], replicated, may hold values from -0.375 to 0.375
- w_down_proj: bfloat16 [128, 4096], replicated, may hold values from -0.5 to 0.5
- w_up_proj: bfloat16 [4096, 128], replicated, may hold values from -0.09375 to 0.09375
- w_up_out: bfloat16 [128, 32], replicated, may hold values from -0.5 to 0.5
- pred_grad: bfloat16 [8, 16, 512], P('sy', 'sx'), may hold values from -0.8984375 to 0.8984375
- text_grad: bfloat16 [8, 32, 4096], P('sy', 'sx'), may hold values from -0.29882812 to 0.29882812
Outputs:
- prediction: bfloat16 [8, 16, 512], P('sy', 'sx')
- text_out: bfloat16 [8, 32, 4096], P('sy', 'sx')
- grad_down_conv: float32 [288, 128], replicated
- grad_down_proj: float32 [128, 4096], replicated
- grad_up_proj: float32 [4096, 128], replicated
- grad_up_out: float32 [128, 32], replicated
All inputs are finite; a program needn't handle non-finite values.
Results may differ from a plain program's by a relative error of at most 0.028.
Values may be sent and summed in bfloat16 or wider, within the bound.
No kernel may reach another device: no remote copies, remote signals or barrier semaphores. Data moves between devices by JAX's collectives and lax.ppermute only.
A program may use at most 192 MiB of HBM per device.

v0:
```python
import math

import jax
import jax.numpy as jnp
from jax import lax
from jax.sharding import PartitionSpec as P

HD = 128


epsilon = 1e-05
NEG_SCORE = -1e30
rope_base = 500000.0


def with_halo(block, sides, width):
    for axis, dim in sides:
        count = lax.axis_size(axis)
        forward = [(i, i + 1) for i in range(count - 1)]
        backward = [(target, source) for source, target in forward]
        low = lax.ppermute(
            lax.slice_in_dim(block, block.shape[dim] - width, None, axis=dim), axis, forward
        )
        high = lax.ppermute(lax.slice_in_dim(block, 0, width, axis=dim), axis, backward)
        block = jnp.concatenate([low, block, high], axis=dim)
    return block


def silu_slope(values):
    sigma = jax.nn.sigmoid(values)
    return sigma * (1.0 + values * (1.0 - sigma))


def neighbour_cells(padded, rows, cols):
    wide = jnp.pad(padded, ((0, 0), (1, 1), (0, 0)))
    parts = [wide[r : r + rows, c : c + cols, :] for r in range(3) for c in range(3)]
    return jnp.concatenate(parts, axis=-1)


def rope_tables(positions, head_size):
    half = head_size // 2
    freq = jnp.exp(-(2.0 * jnp.arange(half, dtype=jnp.float32) / head_size) * math.log(rope_base))
    angle = positions.astype(jnp.float32)[:, None] * freq[None, :]
    return (jnp.cos(angle)[:, None, :], jnp.sin(angle)[:, None, :])


def rotate(values, cosine, sine):
    half = values.shape[-1] // 2
    first = values[..., :half]
    second = values[..., half:]
    return jnp.concatenate(
        [first * cosine - second * sine, second * cosine + first * sine], axis=-1
    )


def shards(
    text_tokens,
    latent,
    image_offset,
    norm_gain,
    w_query,
    w_key,
    w_value,
    w_out,
    w_down_conv,
    w_down_proj,
    w_up_proj,
    w_up_out,
    pred_grad,
    text_grad,
):
    wide_type = jnp.float32
    text_local = text_tokens[0]
    latent_tile = latent[0]
    offset = image_offset[0]
    lat_chan = w_up_out.shape[1]
    text_rows = text_local.shape[0]
    tile_rows = latent_tile.shape[0]
    tile_cols = latent_tile.shape[1] // lat_chan
    image_rows = tile_rows * tile_cols
    share_rows = text_rows + image_rows
    row_groups = lax.axis_size("sx")
    seq_blocks = lax.axis_size("sy")
    block_len = share_rows * row_groups
    image_len = image_rows * row_groups
    total_len = block_len * seq_blocks
    own_block = lax.axis_index("sy")
    head_width = w_query.shape[1]
    heads_here = head_width // HD
    score_scale = HD ** (-0.5)
    rimmed = with_halo(latent_tile, (("sx", 0),), 1)
    grid_cells = rimmed.reshape(tile_rows + 2, tile_cols, lat_chan)
    patches = neighbour_cells(grid_cells, tile_rows, tile_cols).reshape(image_rows, 9 * lat_chan)
    pre_down = jnp.dot(patches, w_down_conv, preferred_element_type=wide_type)
    down_act = jax.nn.silu(pre_down).astype(jnp.bfloat16)
    embedded = jnp.dot(down_act, w_down_proj, preferred_element_type=wide_type).astype(jnp.bfloat16)
    local_rows = jnp.concatenate([text_local, embedded], axis=0)
    gain = norm_gain.astype(wide_type)
    w_project = jnp.concatenate([w_query, w_key, w_value], axis=1)
    inputs = lax.all_gather(local_rows, "sx", axis=0, tiled=True).astype(wide_type)
    inverse = lax.rsqrt(jnp.mean(inputs * inputs, axis=-1, keepdims=True) + epsilon)
    normed = (inputs * inverse * gain).astype(jnp.bfloat16)
    projected = jnp.dot(normed, w_project, preferred_element_type=wide_type)

    def layout(row_ids):
        part_index = row_ids // share_rows
        inner_row = row_ids % share_rows
        is_image = inner_row >= text_rows
        text_index = part_index * text_rows + inner_row
        text_pos = text_index + jnp.where(text_index >= offset, image_len, 0)
        image_pos = offset + part_index * image_rows + (inner_row - text_rows)
        return (jnp.where(is_image, image_pos, text_pos), is_image)

    query_pos, query_image = layout(jnp.arange(block_len, dtype=jnp.int32))
    cosine, sine = rope_tables(own_block * block_len + query_pos, HD)
    queries = rotate(
        projected[:, :head_width].reshape(block_len, heads_here, HD), cosine, sine
    ).astype(jnp.bfloat16)
    keys_turned = (
        rotate(
            projected[:, head_width : 2 * head_width].reshape(block_len, heads_here, HD),
            cosine,
            sine,
        )
        .astype(jnp.bfloat16)
        .reshape(block_len, head_width)
    )
    keys_values = jnp.concatenate(
        [keys_turned, projected[:, 2 * head_width :].astype(jnp.bfloat16)], axis=1
    )

    def visible(key_ids):
        key_block = key_ids // block_len
        key_pos, key_image = layout(key_ids % block_len)
        same = (key_block == own_block)[None, :] & (
            (key_pos[None, :] <= query_pos[:, None]) | key_image[None, :] & query_image[:, None]
        )
        return (key_block < own_block)[None, :] | same

    def stats_keys(running, shard_piece, first_row):
        peak, total = running
        count_rows = shard_piece.shape[0]
        key_heads = shard_piece[:, :head_width].reshape(count_rows, heads_here, HD)
        allowed = visible(first_row + jnp.arange(count_rows, dtype=jnp.int32))
        scores = (
            jnp.einsum("qhd,khd->hqk", queries, key_heads, preferred_element_type=wide_type)
            * score_scale
        )
        scores = jnp.where(allowed[None], scores, NEG_SCORE)
        new_peak = jnp.maximum(peak, jnp.max(scores, axis=-1))
        raised = jnp.where(allowed[None], jnp.exp(scores - new_peak[:, :, None]), 0.0)
        total = total * jnp.exp(peak - new_peak) + jnp.sum(raised, axis=-1)
        return (new_peak, total)

    def stats_visible(running, shard_piece, first_row):
        return stats_keys(running, shard_piece, first_row)

    key_step = math.gcd(total_len, 512)
    slab_count = total_len // key_step
    start_state = (
        jnp.full((heads_here, block_len), NEG_SCORE, wide_type),
        jnp.zeros((heads_here, block_len), wide_type),
    )
    every_key = lax.all_gather(keys_values, "sy", axis=0, tiled=True)

    def stats_turn(index, running):
        first_row = index * key_step
        return stats_visible(
            running, lax.dynamic_slice_in_dim(every_key, first_row, key_step, 0), first_row
        )

    peak, total = lax.fori_loop(0, slab_count, stats_turn, start_state)
    log_total = peak + jnp.log(total)

    def mix_keys(accum, shard_piece, first_row):
        key_heads = shard_piece[:, :head_width].reshape(key_step, heads_here, HD)
        value_heads = shard_piece[:, head_width:].reshape(key_step, heads_here, HD)
        allowed = visible(first_row + jnp.arange(key_step, dtype=jnp.int32))
        scores = (
            jnp.einsum("qhd,khd->hqk", queries, key_heads, preferred_element_type=wide_type)
            * score_scale
        )
        scores = jnp.where(allowed[None], scores, NEG_SCORE)
        probs = jnp.where(allowed[None], jnp.exp(scores - log_total[:, :, None]), 0.0)
        return accum + jnp.einsum(
            "hqk,khd->qhd",
            probs.astype(jnp.bfloat16),
            value_heads,
            preferred_element_type=wide_type,
        )

    def mix_turn(index, accum):
        first_row = index * key_step
        shard_piece = lax.dynamic_slice_in_dim(every_key, first_row, key_step, 0)
        return mix_keys(accum, shard_piece, first_row)

    accum = lax.fori_loop(
        0, slab_count, mix_turn, jnp.zeros((block_len, heads_here, HD), wide_type)
    )
    attended = accum.astype(jnp.bfloat16).reshape(block_len, head_width)
    rows_here = attended
    mixed_rows = lax.psum_scatter(
        jnp.dot(rows_here, w_out, preferred_element_type=wide_type).astype(jnp.bfloat16),
        "sx",
        scatter_dimension=0,
        tiled=True,
    ).astype(jnp.float32)
    layer_out = (local_rows.astype(wide_type) + mixed_rows).astype(jnp.bfloat16)
    text_out = layer_out[:text_rows]
    image_out = layer_out[text_rows:]
    pre_up = jnp.dot(image_out, w_up_proj, preferred_element_type=wide_type)
    up_act = jax.nn.silu(pre_up).astype(jnp.bfloat16)
    prediction = (
        jnp.dot(up_act, w_up_out, preferred_element_type=wide_type)
        .astype(jnp.bfloat16)
        .reshape(tile_rows, tile_cols * lat_chan)
    )
    out_grad = pred_grad[0].reshape(image_rows, lat_chan)
    grad_up_out = jnp.einsum("ru,rc->uc", up_act, out_grad, preferred_element_type=wide_type)
    grad_pre_up = (
        jnp.einsum("rc,uc->ru", out_grad, w_up_out, preferred_element_type=wide_type)
        * silu_slope(pre_up)
    ).astype(jnp.bfloat16)
    grad_up_proj = jnp.einsum("rd,ru->du", image_out, grad_pre_up, preferred_element_type=wide_type)
    grad_image = jnp.einsum("ru,du->rd", grad_pre_up, w_up_proj, preferred_element_type=wide_type)
    grad_rows = jnp.concatenate([text_grad[0].astype(wide_type), grad_image], axis=0).astype(
        jnp.bfloat16
    )
    grad_attended = jnp.einsum(
        "rd,hd->rh",
        lax.all_gather(grad_rows, "sx", axis=0, tiled=True),
        w_out,
        preferred_element_type=wide_type,
    ).astype(jnp.bfloat16)
    grad_heads = grad_attended.reshape(block_len, heads_here, HD)
    delta = jnp.einsum(
        "qhd,qhd->hq",
        grad_heads,
        attended.reshape(block_len, heads_here, HD),
        preferred_element_type=wide_type,
    )

    def back_keys(query_sum, shard_piece, first_row):
        key_heads = shard_piece[:, :head_width].reshape(key_step, heads_here, HD)
        value_heads = shard_piece[:, head_width:].reshape(key_step, heads_here, HD)
        allowed = visible(first_row + jnp.arange(key_step, dtype=jnp.int32))
        scores = (
            jnp.einsum("qhd,khd->hqk", queries, key_heads, preferred_element_type=wide_type)
            * score_scale
        )
        scores = jnp.where(allowed[None], scores, NEG_SCORE)
        probs = jnp.where(allowed[None], jnp.exp(scores - log_total[:, :, None]), 0.0)
        weights = probs.astype(jnp.bfloat16)
        grad_prob = jnp.einsum(
            "qhd,khd->hqk", grad_heads, value_heads, preferred_element_type=wide_type
        )
        grad_score = (probs * (grad_prob - delta[:, :, None]) * score_scale).astype(jnp.bfloat16)
        query_sum = query_sum + jnp.einsum(
            "hqk,khd->qhd", grad_score, key_heads, preferred_element_type=wide_type
        )
        key_part = jnp.einsum(
            "hqk,qhd->khd", grad_score, queries, preferred_element_type=wide_type
        ).astype(jnp.bfloat16)
        value_part = jnp.einsum(
            "hqk,qhd->khd", weights, grad_heads, preferred_element_type=wide_type
        ).astype(jnp.bfloat16)
        return (
            query_sum,
            jnp.concatenate(
                [key_part.reshape(key_step, head_width), value_part.reshape(key_step, head_width)],
                axis=1,
            ),
        )

    def back_turn(query_sum, index):
        first_row = index * key_step
        shard_piece = lax.dynamic_slice_in_dim(every_key, first_row, key_step, 0)
        return back_keys(query_sum, shard_piece, first_row)

    query_sum, key_pieces = lax.scan(
        back_turn,
        jnp.zeros((block_len, heads_here, HD), wide_type),
        jnp.arange(slab_count, dtype=jnp.int32),
    )
    grads_term = key_pieces.reshape(total_len, 2 * head_width)
    own_sums = lax.psum_scatter(
        grads_term.astype(wide_type).astype(jnp.bfloat16), "sy", scatter_dimension=0, tiled=True
    ).astype(jnp.float32)
    grad_query = (
        rotate(query_sum, cosine, -sine).astype(jnp.bfloat16).reshape(block_len, head_width)
    )
    grad_key = (
        rotate(own_sums[:, :head_width].reshape(block_len, heads_here, HD), cosine, -sine)
        .astype(jnp.bfloat16)
        .reshape(block_len, head_width)
    )
    grad_value = own_sums[:, head_width:].astype(jnp.bfloat16)
    head_grads = jnp.concatenate([grad_query, grad_key, grad_value], axis=1)
    rows_here = head_grads
    grad_normed = lax.psum_scatter(
        jnp.einsum("rh,dh->rd", rows_here, w_project, preferred_element_type=wide_type).astype(
            jnp.bfloat16
        ),
        "sx",
        scatter_dimension=0,
        tiled=True,
    ).astype(jnp.float32)
    inputs = local_rows.astype(wide_type)
    inverse = lax.rsqrt(jnp.mean(inputs * inputs, axis=-1, keepdims=True) + epsilon)
    scaled = grad_normed * gain
    grad_in = (
        grad_rows.astype(wide_type)
        + inverse * scaled
        - inputs * inverse**3 * jnp.mean(inputs * scaled, axis=-1, keepdims=True)
    )
    grad_embedded = grad_in[text_rows:].astype(jnp.bfloat16)
    grad_down_proj = jnp.einsum(
        "ru,rd->ud", down_act, grad_embedded, preferred_element_type=wide_type
    )
    grad_pre_down = (
        jnp.einsum("rd,ud->ru", grad_embedded, w_down_proj, preferred_element_type=wide_type)
        * silu_slope(pre_down)
    ).astype(jnp.bfloat16)
    grad_down_conv = jnp.einsum(
        "rc,ru->cu", patches, grad_pre_down, preferred_element_type=wide_type
    )
    weight_sums = lax.psum(
        (grad_down_conv, grad_down_proj, grad_up_proj, grad_up_out), ("sx", "sy")
    )
    return (
        prediction[None],
        text_out[None],
        weight_sums[0],
        weight_sums[1],
        weight_sums[2],
        weight_sums[3],
    )


def solution(mesh):
    placed = (
        P("sy", "sx", None),
        P("sy", "sx", None),
        P("sy"),
        P(),
        P(None, "sx"),
        P(None, "sx"),
        P(None, "sx"),
        P("sx", None),
        P(),
        P(),
        P(),
        P(),
        P("sy", "sx", None),
        P("sy", "sx", None),
    )
    return jax.shard_map(
        shards,
        mesh=mesh,
        in_specs=placed,
        out_specs=(P("sy", "sx", None), P("sy", "sx", None), P(), P(), P(), P()),
        check_vma=False,
    )
```

profile of v0, /device:TPU:0, one launch (start us, length us, event | category | flops | bytes accessed | tf_op | source)
XLA Modules:
  0.0 821.9 jit_solution(11560024827066682676)
XLA Ops:
  9.3 5.6 collective-permute-start
  18.9 1.4 fusion.111
  22.4 7.9 constant_dynamic-update-slice_fusion.3
  30.3 8.1 constant_dynamic-update-slice_fusion.2
  38.3 7.8 constant_dynamic-update-slice_fusion.1
  46.2 14.9 %all-gather.4.cloned.1.call-done = bf16[288,4096]{1,0:T(8,128)(2,1)} async-done(((bf16[72,4096]{1,0:T(8,128)(2,1)}), bf16[288,4096]{1,0:T(8,128)(2,1)}) %all-gather.4.cloned.1.call-update) | async-done | bytes 2359312 | tf_op jit(solution)/shard_map/all_gather | solution.py:100
  61.1 2.4 fusion.64
  63.4 12.3 %fusion.67 = f32[288,3072]{1,0:T(8,128)S(1)} fusion(bf16[4096,3072]{1,0:T(8,128)(2,1)} %constant_dynamic-update-slice_fusion.1, bf16[288,4096]{1,0:T(8,128)(2,1)S(1)} %copy-done.20, f32[4096]{0:T(1024)S(1)} %convert_element_type.140, f32[288]{0:T(512)S(1)} %add_rsqrt_fusion), kind=kOutput, calls=%fused_computation.137 | convolution fusion | flops 7252475904 | bytes 31081600 | tf_op jit(solution)/shard_map/dot_general | solution.py:103
  80.4 89.4 %all-gather.6.cloned.1.call-done = bf16[2304,2048]{1,0:T(8,128)(2,1)} async-done(((bf16[288,2048]{1,0:T(8,128)(2,1)}), bf16[2304,2048]{1,0:T(8,128)(2,1)}) %all-gather.6.cloned.1.call-update) | async-done | bytes 9437200 | tf_op jit(solution)/shard_map/all_gather | solution.py:164
  169.8 12.8 %copy.68 = bf16[2304,2048]{0,1:T(8,128)(2,1)} copy(bf16[2304,2048]{1,0:T(8,128)(2,1)} %all-gather.6.cloned.1.call-done) | data formatting | bytes 18874368
  182.7 42.8 %while.58 = (s32[]{:T(128)}, f32[8,288]{1,0:T(8,128)S(1)}, f32[8,288]{1,0:T(8,128)S(1)}, s32[]{:T(128)}, s32[]{:T(128)}, /*index=5*/bf16[2304,2048]{0,1:T(8,128)...) while((s32[]{:T(128)}, f32[8,288]{1,0:T(8,128)S(1)}, ...), condition=%wide.region_4.5_spmd.clone.clone.clone, body=%wide.region_1.4_spmd.clone.clone.clone.sunk | while | flops 156116416 | bytes 9588262 | solution.py:172
  226.1 55.7 %while.59 = (s32[]{:T(128)}, f32[288,8,128]{2,0,1:T(8,128)}, bf16[2304,2048]{0,1:T(8,128)(2,1)}, s32[]{:T(128)}, s32[]{:T(128)}, /*index=5*/bf16[288,8,128]{2,0,...) while((s32[]{:T(128)}, f32[288,8,128]{2,0,1:T(8,128)}, ...), condition=%wide.region_6.7_spmd.clone.clone.clone, body=%wide.region_5.6_spmd.clone.clone.clone.sunk | while | flops 305920192 | bytes 8617533 | solution.py:197
  226.1 1.3 constant_dynamic-slice_fusion.6
  229.0 2.8 fusion.192
  231.8 1.3 constant_dynamic-slice_fusion.6
  234.7 3.3 fusion.192
  238.0 1.3 constant_dynamic-slice_fusion.6
  240.9 3.3 fusion.192
  244.3 1.3 constant_dynamic-slice_fusion.6
  247.2 3.3 fusion.192
  250.5 1.3 constant_dynamic-slice_fusion.6
  253.5 3.3 fusion.192
  256.8 1.3 constant_dynamic-slice_fusion.6
  259.7 3.3 fusion.192
  263.0 1.3 constant_dynamic-slice_fusion.6
  266.0 3.3 fusion.192
  269.3 1.3 constant_dynamic-slice_fusion.6
  272.2 3.3 fusion.192
  275.6 1.3 constant_dynamic-slice_fusion.6
  278.5 3.3 fusion.192
  281.8 7.8 convolution_convert_fusion.2
  290.4 35.3 %reduce-scatter.10.cloned.1.call-done = bf16[72,4096]{1,0:T(8,128)(2,1)} async-done(((bf16[288,4096]{1,0:T(8,128)(2,1)}), bf16[72,4096]{1,0:T(8,128)(2,1)}) %reduce-scatter.10.cloned.1.call-update) | async-done | bytes 589840
  330.5 37.3 %all-gather.8.cloned.1.call-done = bf16[288,4096]{1,0:T(8,128)(2,1)} async-done(((bf16[72,4096]{1,0:T(8,128)(2,1)}), bf16[288,4096]{1,0:T(8,128)(2,1)}) %all-gather.8.cloned.1.call-update) | async-done | bytes 2359312 | tf_op jit(solution)/shard_map/all_gather | solution.py:231
  367.8 6.7 convolution_convert_fusion.6
  377.1 125.3 %while.60 = (s32[]{:T(128)}, f32[288,8,128]{2,0,1:T(8,128)}, bf16[9,256,2048]{2,1,0:T(8,128)(2,1)}, s32[9]{0:T(128)S(1)}, bf16[2304,2048]{0,1:T(8,128)(2,1)}, /*...) while((s32[]{:T(128)}, f32[288,8,128]{2,0,1:T(8,128)}, ...), condition=%wide.region_10.11_spmd.clone.clone.clone, body=%wide.region_9.10_spmd.clone.clone.clone.sunk | while | flops 763885760 | bytes 54567680 | solution.py:280
  381.5 1.7 fusion.206
  384.6 2.7 fusion.208
  395.0 1.7 fusion.206
  398.2 3.1 fusion.208
  409.0 1.7 fusion.206
  412.2 3.1 fusion.208
  423.0 1.7 fusion.206
  426.1 3.1 fusion.208
  436.9 1.7 fusion.206
  440.1 3.1 fusion.208
  450.9 1.7 fusion.206
  454.1 3.1 fusion.208
  464.8 1.7 fusion.206
  468.0 3.1 fusion.208
  478.8 1.7 fusion.206
  482.0 3.1 fusion.208
  492.8 1.7 fusion.206
  495.9 3.1 fusion.208
  504.3 97.7 %reduce-scatter.8.cloned.1.call-done = bf16[288,2048]{1,0:T(8,128)(2,1)} async-done(((bf16[2304,2048]{1,0:T(8,128)(2,1)}), bf16[288,2048]{1,0:T(8,128)(2,1)}) %reduce-scatter.8.cloned.1.call-update) | async-done | bytes 1179664 | tf_op jit(solution)/shard_map/reduce_scatter | solution.py:286
  602.1 2.2 convert_bitcast_fusion
  607.8 14.1 %convolution_convert_fusion.3 = bf16[288,4096]{1,0:T(8,128)(2,1)} fusion(bf16[4096,3072]{1,0:T(8,128)(2,1)} %constant_dynamic-update-slice_fusion.1, bf16[288,1024]{1,0:T(8,128)(2,1)S(1)} %copy-done.27, bf16[288,1024]{1,0:T(8,128)(2,1)S(1)} %bitcast.230, bf16[288,1024]{1,0:T(8,128)(2,1)S(1)} %bitcast.231), kind=kOutput, calls=%fused_computation.131 | convolution fusion | flops 7254245376 | bytes 29294592 | tf_op jit(solution)/shard_map/rh,dh->rd/dot_general | solution.py:301
  623.0 1.8 fusion.86
  624.8 33.1 %reduce-scatter.12.cloned.1.call-done = bf16[72,4096]{1,0:T(8,128)(2,1)} async-done(((bf16[288,4096]{1,0:T(8,128)(2,1)}), bf16[72,4096]{1,0:T(8,128)(2,1)}) %reduce-scatter.12.cloned.1.call-update) | async-done | bytes 589840
  657.9 1.5 multiply_reduce_fusion.2
  661.8 1.8 fusion.110
  665.4 39.8 %psum.31 = f32[128,32]{0,1:T(8,128)} all-reduce(f32[128,32]{0,1:T(8,128)S(1)} %fusion.115), channel_id=1, replica_groups=mesh['sx'=4,'sy'=8] {'sx','sy'}, use_global_device_ids=true, to_apply=%region_17.18 | all-reduce | flops 4096 | bytes 32768 | tf_op jit(solution)/shard_map/psum | solution.py:327
  705.9 103.1 %all-reduce.6.cloned.1.call-done = (f32[288,128]{1,0:T(8,128)}, f32[128,4096]{1,0:T(8,128)}, f32[4096,128]{1,0:T(8,128)}) async-done(((f32[288,128]{1,0:T(8,128)}, f32[128,4096]{1,0:T(8,128)}, f32[4096,128]{1,0:T(8,128)}), (f32[288,128]{1,0:T(8,128)}, f32[128,4096]{1,0:T(8,128)}, f32[4096,128]{1,0:T(8,128)})) %all-reduce.6.cloned.1.call-update) | async-done | bytes 4341776 | tf_op jit(solution)/shard_map/psum | solution.py:327
  808.9 1.6 copy.147
  810.5 3.3 copy.148
  (587 shorter events, 164.8 us)
Async XLA Ops:
  7.2 11.4 %copy-start = (bf16[128,4096]{1,0:T(8,128)(2,1)S(1)}, bf16[128,4096]{1,0:T(8,128)(2,1)}, u32[]{:S(2)}) copy-start(bf16[128,4096]{1,0:T(8,128)(2,1)} %param.29) | copy-start | bytes 3145732
  7.2 53.9 %all-gather.4.cloned.1.call-start = ((), (), s32[]{:S(2)}) async-start(), calls=%async_computation.3 | async-start | bytes 2949120 | tf_op jit(solution)/shard_map/all_gather | solution.py:100
  8.0 8.5 %collective-permute-start.1 = (bf16[1,512]{1,0:T(2,128)(2,1)S(1)}, bf16[1,512]{1,0:T(2,128)(2,1)S(1)}, u32[]{:S(2)}, u32[]{:S(2)}) collective-permute-start(bf16[1,512]{1,0:T(2,128)(2,1)S(1)} %get-tuple-element.1186), channel_id=1, source_target_pairs={{8,0},{16,8},{24,16},{9,1},{17,9},{25,17},{10,2},{18,10},{26,18},{... | collective-permute-start | bytes 3080 | tf_op jit(solution)/shard_map/ppermute | solution.py:24
  9.3 9.6 %copy-start.25 = (bf16[1,8,4096]{2,1,0:T(8,128)(2,1)S(1)}, bf16[1,8,4096]{2,1,0:T(8,128)(2,1)}, u32[]{:S(2)}) copy-start(bf16[1,8,4096]{2,1,0:T(8,128)(2,1)} %param.20) | copy-start | bytes 196612
  9.3 7.3 collective-permute-start
  16.9 3.4 copy-start.31
  20.4 149.5 %all-gather.6.cloned.1.call-start = ((), (), s32[]{:S(2)}) async-start(), calls=%async_computation.4 | async-start | bytes 10616832 | tf_op jit(solution)/shard_map/all_gather | solution.py:164
  20.4 43.0 %copy-start.36 = (f32[4096]{0:T(1024)}, f32[4096]{0:T(1024)S(1)}, u32[]{:S(2)}) copy-start(f32[4096]{0:T(1024)S(1)} %convert_element_type.140) | copy-start | bytes 49156
  22.4 54.2 %copy-start.22 = (f32[288,64]{1,0:T(8,128)}, f32[288,64]{1,0:T(8,128)S(1)}, u32[]{:S(2)}) copy-start(f32[288,64]{1,0:T(8,128)S(1)} %get-tuple-element.1189) | copy-start | bytes 221188
  61.1 2.4 copy-start.20
  78.9 246.7 %reduce-scatter.10.cloned.1.call-start = ((), (), s32[]{:S(2)}) async-start(), calls=%async_computation.7 | async-start | bytes 2949120
  226.1 2.9 copy-start.4
  231.8 2.9 copy-start.4
  238.0 2.9 copy-start.4
  244.3 2.9 copy-start.4
  250.5 2.9 copy-start.4
  256.8 2.9 copy-start.4
  263.0 2.9 copy-start.4
  269.3 2.9 copy-start.4
  275.5 2.9 copy-start.4
  289.6 36.0 %copy-start.12 = (bf16[64,4096]{1,0:T(8,128)(2,1)S(1)}, bf16[64,4096]{1,0:T(8,128)(2,1)}, u32[]{:S(2)}) copy-start(bf16[64,4096]{1,0:T(8,128)(2,1)} %copy-done.11) | copy-start | bytes 1572868
  289.6 36.0 %copy-start.26 = (bf16[1,8,4096]{2,1,0:T(8,128)(2,1)S(1)}, bf16[1,8,4096]{2,1,0:T(8,128)(2,1)}, u32[]{:S(2)}) copy-start(bf16[1,8,4096]{2,1,0:T(8,128)(2,1)} %param.20) | copy-start | bytes 196612
  289.6 37.2 %copy-start.19 = (bf16[4096,128]{1,0:T(8,128)(2,1)S(1)}, bf16[4096,128]{1,0:T(8,128)(2,1)}, u32[]{:S(2)}) copy-start(bf16[4096,128]{1,0:T(8,128)(2,1)} %param.30) | copy-start | bytes 3145732
  289.7 78.1 %all-gather.8.cloned.1.call-start = ((), (), s32[]{:S(2)}) async-start(), calls=%async_computation.5 | async-start | bytes 2949120 | tf_op jit(solution)/shard_map/all_gather | solution.py:231
  290.4 37.5 %copy-start.39 = (bf16[64,32]{1,0:T(8,128)(2,1)}, bf16[64,32]{1,0:T(8,128)(2,1)S(1)}, u32[]{:S(2)}) copy-start(bf16[64,32]{1,0:T(8,128)(2,1)S(1)} %reshape_squeeze.3) | copy-start | bytes 12292
  328.0 2.2 copy-start.34
  330.2 271.9 %reduce-scatter.8.cloned.1.call-start = ((), (), s32[]{:S(2)}) async-start(), calls=%async_computation.6 | async-start | bytes 10616832 | tf_op jit(solution)/shard_map/reduce_scatter | solution.py:286
  377.1 10.2 %copy-start.7 = (bf16[288,8,128]{2,0,1:T(8,128)(2,1)}, bf16[288,8,128]{2,0,1:T(8,128)(2,1)S(1)}, u32[]{:S(2)}) copy-start(bf16[288,8,128]{2,0,1:T(8,128)(2,1)S(1)} %get-tuple-element.1483) | copy-start | bytes 1769476 | tf_op jit(solution)/shard_map/while
  379.9 3.3 copy-start.9
  384.6 2.7 copy-start.2
  389.1 1.6 copy-start.8
  390.7 10.6 %copy-start.7 = (bf16[288,8,128]{2,0,1:T(8,128)(2,1)}, bf16[288,8,128]{2,0,1:T(8,128)(2,1)S(1)}, u32[]{:S(2)}) copy-start(bf16[288,8,128]{2,0,1:T(8,128)(2,1)S(1)} %get-tuple-element.1483) | copy-start | bytes 1769476 | tf_op jit(solution)/shard_map/while
  393.4 3.3 copy-start.9
  398.2 3.1 copy-start.2
  404.6 10.6 %copy-start.7 = (bf16[288,8,128]{2,0,1:T(8,128)(2,1)}, bf16[288,8,128]{2,0,1:T(8,128)(2,1)S(1)}, u32[]{:S(2)}) copy-start(bf16[288,8,128]{2,0,1:T(8,128)(2,1)S(1)} %get-tuple-element.1483) | copy-start | bytes 1769476 | tf_op jit(solution)/shard_map/while
  407.4 3.3 copy-start.9
  412.2 3.1 copy-start.2
  417.0 1.6 copy-start.8
  418.6 10.6 %copy-start.7 = (bf16[288,8,128]{2,0,1:T(8,128)(2,1)}, bf16[288,8,128]{2,0,1:T(8,128)(2,1)S(1)}, u32[]{:S(2)}) copy-start(bf16[288,8,128]{2,0,1:T(8,128)(2,1)S(1)} %get-tuple-element.1483) | copy-start | bytes 1769476 | tf_op jit(solution)/shard_map/while
  421.4 3.3 copy-start.9
  426.1 3.1 copy-start.2
  432.6 10.6 %copy-start.7 = (bf16[288,8,128]{2,0,1:T(8,128)(2,1)}, bf16[288,8,128]{2,0,1:T(8,128)(2,1)S(1)}, u32[]{:S(2)}) copy-start(bf16[288,8,128]{2,0,1:T(8,128)(2,1)S(1)} %get-tuple-element.1483) | copy-start | bytes 1769476 | tf_op jit(solution)/shard_map/while
  435.3 3.3 copy-start.9
  440.1 3.1 copy-start.2
  446.5 10.6 %copy-start.7 = (bf16[288,8,128]{2,0,1:T(8,128)(2,1)}, bf16[288,8,128]{2,0,1:T(8,128)(2,1)S(1)}, u32[]{:S(2)}) copy-start(bf16[288,8,128]{2,0,1:T(8,128)(2,1)S(1)} %get-tuple-element.1483) | copy-start | bytes 1769476 | tf_op jit(solution)/shard_map/while
  449.3 3.3 copy-start.9
  454.1 3.1 copy-start.2
  460.5 10.6 %copy-start.7 = (bf16[288,8,128]{2,0,1:T(8,128)(2,1)}, bf16[288,8,128]{2,0,1:T(8,128)(2,1)S(1)}, u32[]{:S(2)}) copy-start(bf16[288,8,128]{2,0,1:T(8,128)(2,1)S(1)} %get-tuple-element.1483) | copy-start | bytes 1769476 | tf_op jit(solution)/shard_map/while
  463.3 3.3 copy-start.9
  468.0 3.1 copy-start.2
  474.4 10.6 %copy-start.7 = (bf16[288,8,128]{2,0,1:T(8,128)(2,1)}, bf16[288,8,128]{2,0,1:T(8,128)(2,1)S(1)}, u32[]{:S(2)}) copy-start(bf16[288,8,128]{2,0,1:T(8,128)(2,1)S(1)} %get-tuple-element.1483) | copy-start | bytes 1769476 | tf_op jit(solution)/shard_map/while
  477.2 3.3 copy-start.9
  482.0 3.1 copy-start.2
  488.4 10.6 %copy-start.7 = (bf16[288,8,128]{2,0,1:T(8,128)(2,1)}, bf16[288,8,128]{2,0,1:T(8,128)(2,1)S(1)}, u32[]{:S(2)}) copy-start(bf16[288,8,128]{2,0,1:T(8,128)(2,1)S(1)} %get-tuple-element.1483) | copy-start | bytes 1769476 | tf_op jit(solution)/shard_map/while
  491.2 3.3 copy-start.9
  495.9 3.1 copy-start.2
  502.4 155.5 %reduce-scatter.12.cloned.1.call-start = ((), (), s32[]{:S(2)}) async-start(), calls=%async_computation.8 | async-start | bytes 2949120
  622.0 35.9 %copy-start.13 = (bf16[64,4096]{1,0:T(8,128)(2,1)S(1)}, bf16[64,4096]{1,0:T(8,128)(2,1)}, u32[]{:S(2)}) copy-start(bf16[64,4096]{1,0:T(8,128)(2,1)} %copy-done.11) | copy-start | bytes 1572868
  622.0 35.9 %copy-start.37 = (f32[4096]{0:T(1024)S(1)}, f32[4096]{0:T(1024)}, u32[]{:S(2)}) copy-start(f32[4096]{0:T(1024)} %copy-done.36) | copy-start | bytes 49156
  622.0 186.9 %all-reduce.6.cloned.1.call-start = ((), (), s32[]{:S(2)}) async-start(), calls=%async_computation.9 | async-start | bytes 8683520 | tf_op jit(solution)/shard_map/psum | solution.py:327
  624.8 34.8 %copy-start.17 = (bf16[64,4096]{1,0:T(8,128)(2,1)S(1)}, bf16[64,4096]{1,0:T(8,128)(2,1)}, u32[]{:S(2)}) copy-start(bf16[64,4096]{1,0:T(8,128)(2,1)} %copy-done.16) | copy-start | bytes 1572868
  657.9 1.8 copy-start.18
  663.6 1.6 copy-start.40
  810.5 3.3 copy-start.21
  (54 other events, 67.5 us)
Sparse Core Ops, SparseCore 0:
  20.5 40.5 all-gather.3
  79.1 90.7 all-gather.5
  289.8 35.8 reduce-scatter.9
  330.3 37.4 all-gather.7
  502.5 99.5 reduce-scatter.7
  622.1 35.7 reduce-scatter.11
  664.5 144.3 all-reduce.5
where the time goes:
time: 826 us; the launch traced here: 822 us
  waiting for transfers between devices  411 us (50%)
  matrix products  140 us (17%)
  local copies, waits for them, and re-layouts  130 us (16%)
  other arithmetic  69.9 us (8%)
  blocking collectives  39.8 us (5%)
  between operations  15.3 us (2%)
  loops' own time  8.4 us (1%)
    psum x1, waiting for transfers between devices, shards(): lax.psum((grad_down_conv, grad_down_proj, grad_up_proj, grad_up_out), ('s...  103 us
    reduce_scatter x1, waiting for transfers between devices, shards(): lax.psum_scatter(grads_term.astype(wide_type).astype(jnp.bfloat16), 'sy',...  97.7 us
    all_gather x1, waiting for transfers between devices, shards(): every_key = lax.all_gather(keys_values, 'sy', axis=0, tiled=True)  89.4 us
    unnamed x9, waiting for transfers between devices  68.4 us
    unnamed x90, local copies, waits for them, and re-layouts  45.7 us
    psum x1, blocking collectives, shards(): lax.psum((grad_down_conv, grad_down_proj, grad_up_proj, grad_up_out), ('s...  39.8 us
    all_gather x1, waiting for transfers between devices, shards(): lax.all_gather(grad_rows, 'sx', axis=0, tiled=True)  37.3 us
    select_n x54, other arithmetic, layout(): return (jnp.where(is_image, image_pos, text_pos), is_image)  36.3 us
  transfers between devices with their start and end apart: 9, of which 7 were waited for; matrix products, arithmetic and copies ran while one was open for 4% of the time, Pallas kernels for 0%

commit v1 on v0

v1 whole, which is shorter than its diff:
```python
import math

import jax
import jax.numpy as jnp
import numpy as np
from jax import lax
from jax.experimental import pallas as pl
from jax.experimental.pallas import tpu as pltpu
from jax.sharding import PartitionSpec as P

HD = 128
EPSILON = 1e-05
NEG_SCORE = -1e30
ROPE_BASE = 500000.0
SCALE = HD ** (-0.5)
LOG2E = math.log2(math.e)
LN2 = math.log(2.0)
F32 = jnp.float32
BF16 = jnp.bfloat16
MIB = 1024 * 1024
VMEM_BYTES = 56 * MIB
SMALL_BYTES = 16 * MIB


def dot(left, right):
    return jnp.dot(left, right, preferred_element_type=F32)


def dot_nt(left, right):
    return lax.dot_general(left, right, (((1,), (1,)), ((), ())), preferred_element_type=F32)


def silu_slope(values):
    sigma = jax.nn.sigmoid(values)
    return sigma * (1.0 + values * (1.0 - sigma))


def silu(values):
    return values * jax.nn.sigmoid(values)


def iota(shape, dim):
    return lax.broadcasted_iota(jnp.int32, shape, dim)


def flip(values):
    return values.astype(F32).T.astype(BF16)


def call(kernel, head, inputs, outs, scratch=(), flops=0, after=(), out_kind=None, room=VMEM_BYTES):
    inputs = [(a, "any") for a in after] + list(inputs)
    skip = len(after)

    def spec(array, block):
        if block == "smem":
            return pl.BlockSpec(memory_space=pltpu.SMEM)
        if block == "cols":
            return pl.BlockSpec((array.shape[0], HD), lambda i, h: (0, h[0]))
        if block == "rows":
            return pl.BlockSpec((HD, array.shape[1]), lambda i, h: (h[0], 0))
        if block == "any":
            return pl.BlockSpec(memory_space=pl.ANY)
        if block == "mine":
            return pl.BlockSpec((1,) + array.shape[1:], lambda i, h: (h[1], 0, 0))
        rank = len(array.shape)
        return pl.BlockSpec(array.shape, lambda i, h: (0,) * rank)

    moved = sum(math.prod(a.shape) * a.dtype.itemsize for a in outs) + sum(
        math.prod(a.shape) * a.dtype.itemsize // (a.shape[1 if b == "cols" else 0] // HD if b in ("cols", "rows") else 1)
        for a, b in inputs
    )
    return pl.pallas_call(
        lambda head_ref, *refs: kernel(head_ref, *refs[skip:]),
        out_shape=outs,
        grid_spec=pltpu.PrefetchScalarGridSpec(
            num_scalar_prefetch=1,
            grid=(1,),
            in_specs=[spec(a, b) for a, b in inputs],
            out_specs=[spec(a, out_kind) for a in outs],
            scratch_shapes=list(scratch),
        ),
        compiler_params=pltpu.CompilerParams(vmem_limit_bytes=room),
        cost_estimate=pl.CostEstimate(flops=flops, bytes_accessed=moved, transcendentals=0),
    )(head, *[a for a, _ in inputs])


def weights_kernel(
    head, wq, wk, wv, wo, gain, w_down, w_up, w_conv,
    proj, proj_t, mapped, u, gram, z, conv_t,
    proj_sum, u_sum, gram_sum, z_sum,
):
    step = pl.program_id(0)
    down = w_down[...]
    scaled = (down.astype(F32) * gain[...].astype(F32)).astype(BF16)
    terms = [(proj_sum.at[n], dot(scaled, w[...])) for n, w in enumerate((wq, wk, wv))]
    terms += [(u_sum, dot(wo[...], w_up[...])), (gram_sum, dot_nt(down, down)), (z_sum, dot(down, w_up[...]))]

    @pl.when(step == 0)
    def _():
        for total, term in terms:
            total[...] = term

    @pl.when(step > 0)
    def _():
        for total, term in terms:
            total[...] += term

    @pl.when(step == pl.num_programs(0) - 1)
    def _():
        for n in range(3):
            cols = slice(n * HD, (n + 1) * HD)
            proj[:, cols] = proj_sum[n].astype(BF16)
            proj_t[cols, :] = proj_sum[n].T.astype(BF16)
            mapped[:, cols] = proj_sum[n].astype(BF16)
        for n in range(2):
            mapped[:, (3 + n) * HD : (4 + n) * HD] = pltpu.roll(proj_sum[n], HD // 2, 1).astype(BF16)
        u[...] = u_sum[...].astype(BF16)
        gram[...] = gram_sum[...].astype(BF16)
        z[...] = z_sum[...].astype(BF16)
        conv_t[...] = flip(w_conv[...])


def small_products(place, wq, wk, wv, wo, gain, w_down, w_up, w_conv):
    rank, width = w_down.shape
    up_chan = w_up.shape[1]
    step_rows = math.gcd(width, 1024)
    cols = pl.BlockSpec((step_rows, HD), lambda i, p: (i, p[0]))
    outs = [(rank, 3 * HD), (3 * HD, rank), (rank, 5 * HD), (HD, up_chan), (rank, rank), (rank, up_chan), w_conv.shape[::-1]]
    return pl.pallas_call(
        weights_kernel,
        out_shape=[jax.ShapeDtypeStruct(shape, BF16) for shape in outs],
        grid_spec=pltpu.PrefetchScalarGridSpec(
            num_scalar_prefetch=1,
            grid=(width // step_rows,),
            in_specs=[cols, cols, cols, pl.BlockSpec((HD, step_rows), lambda i, p: (p[0], i)),
                      pl.BlockSpec((1, step_rows), lambda i, p: (0, i)), pl.BlockSpec((rank, step_rows), lambda i, p: (0, i)),
                      pl.BlockSpec((step_rows, up_chan), lambda i, p: (i, 0)), pl.BlockSpec(w_conv.shape, lambda i, p: (0, 0))],
            out_specs=[pl.BlockSpec(shape, lambda i, p: (0, 0)) for shape in outs],
            scratch_shapes=[pltpu.VMEM((3, rank, HD), F32), pltpu.VMEM((HD, up_chan), F32),
                            pltpu.VMEM((rank, rank), F32), pltpu.VMEM((rank, up_chan), F32)],
        ),
        compiler_params=pltpu.CompilerParams(vmem_limit_bytes=SMALL_BYTES),
        cost_estimate=pl.CostEstimate(flops=4_000_000_000, bytes_accessed=12 * HD * width, transcendentals=0),
    )(place, wq, wk, wv, wo, gain, w_down, w_up, w_conv)


def pick(rows, total, spot):
    return (iota((total, rows), 0) == iota((total, rows), 1) + spot).astype(BF16)


def gathered(parts, group):
    rows = parts[0].shape[0]
    total = rows * len(parts)
    return sum(dot(pick(rows, total, (group ^ k) * rows), part[...]) for k, part in enumerate(parts))


def text_kernel(count, place, *refs):
    parts = refs[:count]
    gain, wq, wk, wv, _, out, normed, sums = refs[count:]
    step = pl.program_id(0)
    rows = wq.shape[0]

    @pl.when(step == 0)
    def _():
        x = gathered(parts, place[2])
        inverse = lax.rsqrt(jnp.mean(x * x, axis=-1, keepdims=True) + EPSILON)
        whole = (x * inverse * gain[...].astype(F32)).astype(BF16)
        for at in range(normed.shape[0]):
            normed[at] = whole[:, at * rows : (at + 1) * rows]
        sums[...] = jnp.zeros_like(sums)

    here = normed[step]
    for n, w in enumerate((wq, wk, wv)):
        sums[n] += dot(here, w[...])

    @pl.when(step == pl.num_programs(0) - 1)
    def _():
        for h in range(out.shape[0]):
            for n in range(3):
                out[h, :, n * HD : (n + 1) * HD] = sums[n, :, h * HD : (h + 1) * HD].astype(BF16)


def text_heads(place, parts, gain, wq, wk, wv, after):
    rows, width = parts[0].shape
    rows *= len(parts)
    wide = wq.shape[1]
    heads = wide // HD
    step_rows = math.gcd(width, 512)
    strip = pl.BlockSpec((step_rows, wide), lambda i, p: (i, 0))
    whole = lambda a: pl.BlockSpec(a.shape, lambda i, p: (0, 0))
    return pl.pallas_call(
        lambda *refs: text_kernel(len(parts), *refs),
        out_shape=jax.ShapeDtypeStruct((heads, rows, 3 * HD), BF16),
        grid_spec=pltpu.PrefetchScalarGridSpec(
            num_scalar_prefetch=1,
            grid=(width // step_rows,),
            in_specs=[whole(a) for a in parts] + [whole(gain), strip, strip, strip, pl.BlockSpec(memory_space=pl.ANY)],
            out_specs=pl.BlockSpec((heads, rows, 3 * HD), lambda i, p: (0, 0, 0)),
            scratch_shapes=[pltpu.VMEM((width // step_rows, rows, step_rows), BF16), pltpu.VMEM((3, rows, wide), F32)],
        ),
        compiler_params=pltpu.CompilerParams(vmem_limit_bytes=VMEM_BYTES),
        cost_estimate=pl.CostEstimate(
            flops=6 * rows * width * wide, bytes_accessed=6 * width * wide, transcendentals=0
        ),
    )(place, *parts, gain, wq, wk, wv, after)


def text_grad_kernel(count, place, *refs):
    parts = refs[:count]
    wo, mix, _ = refs[count : count + 3]
    outs = refs[count + 3 : -1]
    grad_t = refs[-1]
    step = pl.program_id(0)

    @pl.when(step == 0)
    def _():
        grad_t[...] = gathered(parts, place[2]).T.astype(BF16)

    back = dot(wo[...], grad_t[...]).T.astype(BF16)
    for k, out in enumerate(outs):

        @pl.when(step == k)
        def _():
            out[:, :HD] = back
            out[:, HD:] = mix[...]


def text_grad_heads(place, parts, wo, mix, repeat, after):
    rows, width = parts[0].shape
    rows *= len(parts)
    peers = mix.shape[0] // rows
    return pl.pallas_call(
        lambda *refs: text_grad_kernel(len(parts), *refs),
        out_shape=[jax.ShapeDtypeStruct((rows, 2 * HD), BF16)] * peers,
        grid_spec=pltpu.PrefetchScalarGridSpec(
            num_scalar_prefetch=1,
            grid=(peers,),
            in_specs=[pl.BlockSpec(a.shape, lambda i, p: (0, 0)) for a in parts]
            + [pl.BlockSpec((HD, width), lambda i, p: ((p[5] ^ i) // repeat, 0)),
               pl.BlockSpec((rows, HD), lambda i, p: (p[5] ^ i, 0)), pl.BlockSpec(memory_space=pl.ANY)],
            out_specs=[pl.BlockSpec((rows, 2 * HD), lambda i, p: (0, 0))] * peers,
            scratch_shapes=[pltpu.VMEM((width, rows), BF16)],
        ),
        compiler_params=pltpu.CompilerParams(vmem_limit_bytes=VMEM_BYTES),
        cost_estimate=pl.CostEstimate(
            flops=2 * rows * width * peers * HD, bytes_accessed=2 * width * peers * HD, transcendentals=0
        ),
    )(place, *parts, wo, mix, after)


def text_out_kernel(repeat, peers, place, *refs):
    mixes = refs[:peers]
    wo = refs[peers]
    outs = refs[peers + 1 :]
    total = 0.0
    for k, mix in enumerate(mixes):
        peer = place[5] ^ k
        rows = pl.ds(pl.multiple_of(peer // repeat * HD, HD), HD)
        counts = jnp.where(peer % repeat == 0, 1.0, 0.0)
        total = total + dot(mix[:, HD:], wo[rows, :]) * counts
    whole = total.astype(BF16)
    for k, out in enumerate(outs):
        rows = out.shape[0]
        out[...] = dot(pick(rows, whole.shape[0], (place[2] ^ k) * rows).astype(F32).T.astype(BF16), whole).astype(BF16)


def text_out_parts(place, mixes, wo, repeat, groups):
    rows = mixes[0].shape[0]
    deep, width = wo.shape
    peers = len(mixes)
    few = rows // groups
    step_cols = math.gcd(width, 1024)
    return pl.pallas_call(
        lambda *refs: text_out_kernel(repeat, peers, *refs),
        out_shape=[jax.ShapeDtypeStruct((few, width), BF16)] * groups,
        grid_spec=pltpu.PrefetchScalarGridSpec(
            num_scalar_prefetch=1,
            grid=(width // step_cols,),
            in_specs=[pl.BlockSpec(a.shape, lambda i, p: (0, 0)) for a in mixes]
            + [pl.BlockSpec((deep, step_cols), lambda i, p: (0, i))],
            out_specs=[pl.BlockSpec((few, step_cols), lambda i, p: (0, i))] * groups,
        ),
        compiler_params=pltpu.CompilerParams(vmem_limit_bytes=SMALL_BYTES),
        cost_estimate=pl.CostEstimate(
            flops=2 * rows * width * peers * HD, bytes_accessed=2 * width * peers * HD, transcendentals=0
        ),
    )(place, *mixes, wo)


def turned(values, cos, sin):
    return values * cos + pltpu.roll(values, HD // 2, 1) * sin


def rope_tables(positions):
    half = HD // 2
    freq = np.exp(-(2.0 * np.arange(half) / HD) * math.log(ROPE_BASE)).astype(np.float32)
    angle = np.asarray(positions, np.float64)[:, None] * np.concatenate([freq, freq])[None].astype(np.float64)
    sign = np.where(np.arange(HD) < half, -1.0, 1.0)[None]
    return np.stack([np.cos(angle), np.sin(angle) * sign]).astype(np.float32)


def angles(cos_start, sin_start, steps):
    return cos_start * steps[0] - sin_start * steps[1], sin_start * steps[0] + cos_start * steps[1]


def start_row(starts, thr, b, extra):
    row = pl.ds(thr[b] + b * extra, 1)
    return starts[0, row, :], starts[1, row, :]


def image_kernel(high, wide, width, extra, thr, lat_t, cell, conv_t, proj_t, mapped, gram, starts, steps, steps_t, _,
                 pre_down, act_t, patch_t, q_img, qt, k_img, kt, v_img, vt):
    chan = lat_t.shape[0]
    lat = lat_t[...]
    row = cell[0:1, :]
    col = cell[1:2, :]
    for r in range(3):
        for c in range(3):
            tap = r * 3 + c
            step = (r - 1) * wide + (c - 1)
            moved = pltpu.roll(lat, -step % lat.shape[1], 1) if step else lat
            keep = (row + (r - 1) >= 0) & (row + (r - 1) < high)
            keep &= (col + (c - 1) >= 0) & (col + (c - 1) < wide)
            patch_t[0, tap * chan : (tap + 1) * chan, :] = jnp.where(keep, moved, 0.0).astype(BF16)
    cos_start, sin_start = start_row(starts, thr, pl.program_id(0), extra)
    before_t = dot(conv_t[...], patch_t[0])
    flat_t = silu(before_t).astype(BF16)
    act_t[0] = flat_t
    square = jnp.sum(dot(gram[...], flat_t) * flat_t.astype(F32), axis=0, keepdims=True)
    inv = lax.rsqrt(square * (1.0 / width) + EPSILON)
    heads_t = dot(proj_t[...], flat_t) * inv
    half = HD // 2
    column = lambda values: jnp.broadcast_to(values, (8, HD)).T[half:, :1]
    cos, sin = angles(column(cos_start), column(sin_start), steps_t)
    for at, out, scale in ((0, qt, SCALE * LOG2E), (HD, kt, 1.0)):
        first = heads_t[at : at + half]
        second = heads_t[at + half : at + HD]
        out[0, :half, :] = ((first * cos - second * sin) * scale).astype(BF16)
        out[0, half:, :] = ((second * cos + first * sin) * scale).astype(BF16)
    vt[0] = heads_t[2 * HD :].astype(BF16)
    before = before_t.T
    pre_down[0] = before
    act = silu(before).astype(BF16)
    square = jnp.sum(dot(act, gram[...]) * act.astype(F32), axis=-1, keepdims=True)
    inv = lax.rsqrt(square * (1.0 / width) + EPSILON)
    heads = dot(act, mapped[...])
    cos, sin = angles(cos_start, sin_start, steps)
    cos = cos * inv
    sin = sin * inv
    query = heads[:, :HD] * cos + heads[:, 3 * HD : 4 * HD] * sin
    q_img[0] = (query * (SCALE * LOG2E)).astype(BF16)
    k_img[0] = (heads[:, HD : 2 * HD] * cos + heads[:, 4 * HD :] * sin).astype(BF16)
    v_img[0] = (heads[:, 2 * HD : 3 * HD] * inv).astype(BF16)


def image_rows(sizes, thr, lat_t, cell, conv_t, proj_t, mapped, gram, starts, steps, steps_t, after):
    blocks = thr.shape[0]
    length = steps.shape[1]
    chan = lat_t.shape[0]
    down_chan, taps = conv_t.shape
    whole = lambda a: pl.BlockSpec(a.shape, lambda b: (0,) * len(a.shape))
    outs = [(length, down_chan, F32), (down_chan, length, BF16), (taps, length, BF16), (length, HD, BF16),
            (HD, length, BF16), (length, HD, BF16), (HD, length, BF16), (length, HD, BF16), (HD, length, BF16)]
    return pl.pallas_call(
        lambda *refs: image_kernel(*sizes, *refs),
        out_shape=[jax.ShapeDtypeStruct((blocks, r, c), kind) for r, c, kind in outs],
        grid=(blocks,),
        in_specs=[pl.BlockSpec(memory_space=pltpu.SMEM), pl.BlockSpec((chan, length), lambda b: (0, b))]
        + [whole(a) for a in (cell, conv_t, proj_t, mapped, gram, starts, steps, steps_t)]
        + [pl.BlockSpec(memory_space=pl.ANY)],
        out_specs=[pl.BlockSpec((1, r, c), lambda b: (b, 0, 0)) for r, c, _ in outs],
        compiler_params=pltpu.CompilerParams(vmem_limit_bytes=SMALL_BYTES),
        cost_estimate=pl.CostEstimate(flops=8_000_000_000, bytes_accessed=8_000_000, transcendentals=0),
    )(thr, lat_t, cell, conv_t, proj_t, mapped, gram, starts, steps, steps_t, after)


def attend_kernel(
    head, thr, text, near, far, qt, k_img, vt, u,
    part, q_txt, qt_txt, k_txt, kt_txt, mix_t, mix_txt_t, mix_txt, lse, lse_txt,
    scores, vt_txt, acc, peak, total,
):
    blocks, length, _ = k_img.shape
    text_total = q_txt.shape[0]
    row = iota((text_total, 1), 0)
    rows = text_total // blocks
    shifted = row >= sum(jnp.where(row // rows == b, thr[b], 0) for b in range(blocks))
    cos = jnp.where(shifted, far[0], near[0])
    sin = jnp.where(shifted, far[1], near[1])
    query = turned(text[:, :HD].astype(F32), cos, sin) * (SCALE * LOG2E)
    q_txt[...] = query.astype(BF16)
    qt_txt[...] = query.T.astype(BF16)
    key = turned(text[:, HD : 2 * HD].astype(F32), cos, sin)
    k_txt[...] = key.astype(BF16)
    kt_txt[...] = key.T.astype(BF16)
    vt_txt[...] = flip(text[:, 2 * HD :])

    def pair(j, _):
        mates = (j, blocks - 1 - j)
        seen = [iota((text_total, length), 0) < thr[i] for i in mates]
        for side, i in enumerate(mates):
            s = jnp.where(seen[side], dot(k_txt[...], qt[i]), NEG_SCORE)
            scores[blocks + 1 + side, :text_total, :length] = s
            peak[side] = jnp.max(s, axis=0, keepdims=True)
        turns = []
        for c in range(blocks + 1):
            first = c <= j
            side = jnp.where(first, 0, 1)
            turns.append((side, jnp.where(first, j, blocks - 1 - j), jnp.where(first, c, c - j - 1)))
        for c, (side, i, key) in enumerate(turns):
            s = dot(k_img[key], qt[i])
            scores[c, :length, :length] = s
            peak[side] = jnp.maximum(peak[side], jnp.max(s, axis=0, keepdims=True))
        for side, i in enumerate(mates):
            p = jnp.where(seen[side], jnp.exp2(scores[blocks + 1 + side, :text_total, :length] - peak[side]), 0.0)
            total[side] = jnp.sum(p, axis=0, keepdims=True)
            acc[side] = dot(vt_txt[...], p.astype(BF16))
        for c, (side, i, key) in enumerate(turns):
            p = jnp.exp2(scores[c, :length, :length] - peak[side])
            total[side] = total[side] + jnp.sum(p, axis=0, keepdims=True)
            acc[side] = acc[side] + dot(vt[key], p.astype(BF16))
        for side, i in enumerate(mates):
            mixed = acc[side] / total[side]
            lse[i] = peak[side] + jnp.log2(total[side])
            mix_t[i] = mixed.astype(BF16)
            part[i] = dot(mixed.T.astype(BF16), u[...]).astype(part.dtype)
        return 0

    lax.fori_loop(0, blocks // 2, pair, 0)

    query = qt_txt[...]
    causal = iota((text_total, text_total), 0) <= iota((text_total, text_total), 1)
    lane = iota((1, text_total), 1)
    s = jnp.where(causal, dot(k_txt[...], query), NEG_SCORE)
    s_list = [s]
    top = jnp.max(s, axis=0, keepdims=True)
    for c in range(blocks):
        s = jnp.where(lane >= thr[c], dot(k_img[c], query), NEG_SCORE)
        scores[c, :length, :text_total] = s
        top = jnp.maximum(top, jnp.max(s, axis=0, keepdims=True))
    p = jnp.where(causal, jnp.exp2(s_list[0] - top), 0.0)
    whole = jnp.sum(p, axis=0, keepdims=True)
    mixed = dot(vt_txt[...], p.astype(BF16))
    for c in range(blocks):
        p = jnp.where(lane >= thr[c], jnp.exp2(scores[c, :length, :text_total] - top), 0.0)
        whole = whole + jnp.sum(p, axis=0, keepdims=True)
        mixed = mixed + dot(vt[c], p.astype(BF16))
    mixed = mixed / whole
    lse_txt[...] = top + jnp.log2(whole)
    mix_txt_t[...] = mixed.astype(BF16)
    mix_txt[...] = mixed.T.astype(BF16)


def up_kernel(head, parts, pre_down, z, w_up_out, preds, grad_copies, prediction, grad_out_t):
    act = silu(pre_down[0]).astype(BF16)
    pre_up = dot(act, z[...])
    for p in range(parts.shape[0]):
        pre_up = pre_up + parts[p].astype(F32)
    up_act = silu(pre_up).astype(BF16)
    grad = (dot_nt(preds[...], w_up_out[...]) * silu_slope(pre_up)).astype(BF16)
    for p in range(parts.shape[0]):
        grad_copies[p] = grad
    prediction[...] = dot(up_act, w_up_out[...]).astype(BF16)
    grad_out_t[...] = dot(flip(preds[...]), up_act)


def piece_spot(place, groups, pairs, number):
    group = number // (2 * pairs) ^ place[2]
    pair = number // 2 % pairs ^ place[3]
    return group, pair, number % 2 ^ place[4]


def put_piece(place, lay, number, rows, values):
    _, groups, pairs, _, _ = lay.shape
    group, pair, core = piece_spot(place, groups, pairs, number)
    lay[core, group, pair, rows, :] = values


def hand_out(lay, sems, keep, send):
    moves = [pltpu.make_async_copy(lay.at[n], out, sems.at[n]) for n, out in enumerate((keep, send))]
    for move in moves:
        move.start()
    for move in moves:
        move.wait()


def add_core_kernel(keep, received, *outs):
    for k, out in enumerate(outs):
        out[...] = (keep[k].astype(F32) + received[k].astype(F32)).astype(BF16)


def add_sx_kernel(count, *refs):
    for m, out in enumerate(refs[count:]):
        out[...] = sum(r[m].astype(F32) for r in refs[:count]).astype(BF16)


def add_kernel(*refs):
    refs[-1][...] = sum(r[...].astype(F32) for r in refs[:-1]).astype(BF16)


def unpack_kernel(groups, pairs, own, place, *refs):
    count = 2 * groups
    grad_conv, grad_down, grad_up, grad_out_t, rest = refs[count:]
    few = refs[0].shape[1] - 2 * own
    per = HD // own
    for n, part in enumerate(refs[:count]):
        for m in range(pairs):
            number = ((place[2] ^ n % groups) * pairs + (place[3] ^ m)) * 2 + (place[4] ^ n // groups)
            grad_up[pl.ds(pl.multiple_of(number * own, own), own), :] = part[m, :own, :].astype(F32)
            cols = pl.ds(pl.multiple_of(number // per * HD, HD), HD)
            rows = pl.ds(pl.multiple_of(number % per * own, own), own)
            grad_down[rows, cols] = part[m, own : 2 * own, :].astype(F32)
            rest[pl.ds(pl.multiple_of(number * few, few), few), :] = part[m, 2 * own :, :].astype(F32)
    taps = grad_conv.shape[0]
    grad_conv[...] = rest[:taps, :]
    grad_out_t[...] = rest[taps : taps + grad_out_t.shape[0], :]


def plain(kernel, inputs, outs, after=()):
    whole = lambda a: pl.BlockSpec(a.shape, lambda: (0,) * len(a.shape))
    moved = sum(math.prod(a.shape) * a.dtype.itemsize for a in list(inputs) + list(outs))
    return pl.pallas_call(
        lambda *refs: kernel(*refs[: len(inputs)], *refs[len(inputs) + len(after) :]),
        out_shape=outs,
        in_specs=[whole(a) for a in inputs] + [pl.BlockSpec(memory_space=pl.ANY) for _ in after],
        out_specs=[whole(a) for a in outs],
        compiler_params=pltpu.CompilerParams(vmem_limit_bytes=SMALL_BYTES),
        cost_estimate=pl.CostEstimate(flops=0, bytes_accessed=moved, transcendentals=0),
    )(*inputs, *after)


def backward_kernel(
    share, copies, extra, place, thr, grad_pre, q_img, qt, k_img, kt, v_img, q_txt, qt_txt, k_txt, kt_txt,
    text, mix_t, mix_txt_t, lse, lse_txt, u, proj, gram, z, gain, starts, steps, grad_out_t, *refs,
):
    blocks, length, _ = q_img.shape
    backs = refs[:blocks]
    (pre_down_far, act_t_far, patch_t_far, wq_far, wk_far, wv_far, wo_far, w_up_far, w_down_far,
     keep, send,
     dq, dk, dv, d_out, d_t, dq_t, d_txt, cross_sum, small_sum,
     pre_down, act_t, patch_t, wq, wk, wv, wo, w_up, w_down, lay, sems) = refs[blocks:]
    text_total = q_txt.shape[0]
    width = w_down.shape[1]
    cols = pl.ds(pl.multiple_of(place[0] * HD, HD), HD)
    moves = [(pre_down_far, pre_down), (act_t_far, act_t), (patch_t_far, patch_t), (wq_far.at[:, cols], wq),
             (wk_far.at[:, cols], wk), (wv_far.at[:, cols], wv), (wo_far.at[cols, :], wo), (w_up_far, w_up),
             (w_down_far, w_down)]
    moves = [pltpu.make_async_copy(far, near, sems.at[n]) for n, (far, near) in enumerate(moves)]
    for move in moves:
        move.start()
    cross_sum[...] = jnp.zeros_like(cross_sum)
    small_sum[...] = jnp.zeros_like(small_sum)
    v_txt = text[:, 2 * HD :]
    rows = text_total // blocks
    for k, back in enumerate(backs):
        d_txt[pl.ds(pl.multiple_of((place[5] ^ k) * rows, rows), rows), :] = back[:, :HD]
    d_txt_t = d_txt[...].astype(F32).T
    delta_txt = jnp.sum(d_txt_t * mix_txt_t[...].astype(F32), axis=0, keepdims=True)
    d_txt_t = d_txt_t.astype(BF16)
    lane = iota((1, text_total), 1)
    for c in range(blocks):
        p = jnp.where(lane >= thr[c], jnp.exp2(dot(k_img[c], qt_txt[...]) - lse_txt[...]), 0.0)
        ds = p * (dot(v_img[c], d_txt_t) - delta_txt)
        dk[c] = dot(ds.astype(BF16), q_txt[...])
        dv[c] = dot(p.astype(BF16), d_txt[...])

    def pair(j, _):
        mates = (j, blocks - 1 - j)
        delta = []
        for side, i in enumerate(mates):
            grad = grad_pre[i]
            cross_sum[...] += dot(mix_t[i], grad)
            d_out[side] = dot_nt(grad, u[...]).astype(BF16)
            turned_grad = dot_nt(u[...], grad).astype(BF16)
            d_t[side] = turned_grad
            delta.append(jnp.sum(turned_grad.astype(F32) * mix_t[i].astype(F32), axis=0, keepdims=True))
        for side, i in enumerate(mates):
            seen = iota((text_total, length), 0) < thr[i]
            p = jnp.where(seen, jnp.exp2(dot(k_txt[...], qt[i]) - lse[i]), 0.0)
            ds = p * (dot(v_txt, d_t[side]) - delta[side])
            dq_t[side] = dot(kt_txt[...], ds.astype(BF16))
        for c in range(blocks + 1):
            first = c <= j
            side = jnp.where(first, 0, 1)
            i = jnp.where(first, j, blocks - 1 - j)
            key = jnp.where(first, c, c - j - 1)
            p = jnp.exp2(dot(k_img[key], qt[i]) - lse[i])
            ds = (p * (dot(v_img[key], d_t[side]) - jnp.where(first, delta[0], delta[1]))).astype(BF16)
            dv[key] = dv[key] + dot(p.astype(BF16), d_out[side])
            dk[key] = dk[key] + dot(ds, q_img[i])
            dq_t[side] = dq_t[side] + dot(kt[key], ds)
        for side in range(2):
            dq[mates[side]] = dq_t[side].T
        return 0

    lax.fori_loop(0, blocks // 2, pair, 0)
    for move in moves:
        move.wait()
    taps = patch_t.shape[1]

    def block(b, query):
        cos, sin = angles(*start_row(starts, thr, b, extra), steps)

        def back(values):
            return values * cos - pltpu.roll(values, HD // 2, 1) * sin

        before = pre_down[b]
        act = silu(before).astype(BF16)
        act_wide = act.astype(F32)
        image = dot(act, gram[...])
        square = jnp.sum(image * act_wide, axis=-1, keepdims=True)
        inv = lax.rsqrt(square * (1.0 / width) + EPSILON)
        heads = jnp.concatenate(
            [back(query) * (inv * SCALE), back(dk[b]) * (inv * LN2), dv[b] * inv], axis=1
        ).astype(BF16)
        lift = dot_nt(heads, proj[...])
        crow = inv * inv * (jnp.sum(act_wide * lift, axis=-1, keepdims=True) * (1.0 / width))
        grad = grad_pre[b]
        d_act = (lift - crow * image) * copies + dot_nt(grad, z[...]) * share
        slope = (d_act * silu_slope(before)).astype(BF16)
        flipped = act_t[b]
        return (
            dot(patch_t[b], slope),
            dot(flipped, heads),
            dot(flipped, (act_wide * crow).astype(BF16)),
            dot(flipped, grad),
        )

    def step(n, carry):
        for b in (n, blocks // 2 + n):
            conv, *more = block(b, dq[b])
            small_sum[:taps, :] += conv
            carry = tuple(a + m for a, m in zip(carry, more))
        return carry

    rank = act_t.shape[1]
    spread, pull, inner = lax.fori_loop(
        0, blocks // 2, step,
        (jnp.zeros((rank, 3 * HD), F32), jnp.zeros((rank, rank), F32), jnp.zeros((rank, grad_pre.shape[2]), F32)),
    )
    spread = (spread * copies).astype(BF16)
    pull = (pull * copies).astype(BF16)
    cross = (cross_sum[...] * copies).T.astype(BF16)
    inner_t = (inner * share).T.astype(BF16)
    inner = (inner * share).astype(BF16)
    small_sum[taps : taps + grad_out_t.shape[0], :] = grad_out_t[...]
    _, groups, pairs, rows, _ = lay.shape
    own = width // (2 * groups * pairs)
    few = rows - 2 * own
    for at in range(0, width, HD):
        cols = slice(at, at + HD)
        down = dot_nt(spread[:, :HD], wq[cols, :]) + dot_nt(spread[:, HD : 2 * HD], wk[cols, :])
        down = (down + dot_nt(spread[:, 2 * HD :], wv[cols, :])) * gain[:, cols].astype(F32)
        down = (down - dot(pull, w_down[:, cols]) + dot_nt(inner, w_up[cols, :])).astype(BF16)
        up = (dot(cross, wo[:, cols]) + dot(inner_t, w_down[:, cols])).T.astype(BF16)
        for part in range(0, HD, own):
            put_piece(place, lay, (at + part) // own, slice(0, own), up[part : part + own])
            put_piece(place, lay, (at + part) // own, slice(own, 2 * own), down[part : part + own])
    for number in range(2 * groups * pairs):
        put_piece(place, lay, number, slice(2 * own, rows), small_sum[number * few : (number + 1) * few, :].astype(BF16))
    hand_out(lay, sems, keep, send)


def shards(
    text_tokens,
    latent,
    image_offset,
    norm_gain,
    w_query,
    w_key,
    w_value,
    w_out,
    w_down_conv,
    w_down_proj,
    w_up_proj,
    w_up_out,
    pred_grad,
    text_grad,
):
    axes = ("sy", "sx")
    text_local = text_tokens[0]
    text_rows, width = text_local.shape
    lat_chan = w_up_out.shape[1]
    up_chan = w_up_proj.shape[1]
    down_chan = w_down_conv.shape[1]
    taps = w_down_conv.shape[0]
    tile_rows = latent.shape[1]
    tile_cols = latent.shape[2] // lat_chan
    row_groups = lax.axis_size("sx")
    blocks = lax.axis_size("sy")
    devices = row_groups * blocks
    high = tile_rows * row_groups
    length = high * tile_cols
    text_block = text_rows * row_groups
    text_total = text_block * blocks
    total = length * blocks
    block_len = length + text_block
    heads_here = w_query.shape[1] // HD
    repeat = blocks // heads_here
    assert heads_here * repeat == blocks and blocks % 2 == 0
    own = lax.axis_index("sy")
    share = 1.0 / devices
    copies = 1.0 / repeat

    device = own * row_groups + lax.axis_index("sx").astype(jnp.int32)
    group = lax.axis_index("sx").astype(jnp.int32)
    own = own.astype(jnp.int32)
    head = jnp.stack([own // repeat, device, group, own // 2, own % 2, own])

    def spread_over(values, axis, count):
        return lax.all_to_all(jnp.broadcast_to(values[None], (count,) + values.shape), axis, 0, 0)

    tag = jnp.broadcast_to(image_offset.astype(BF16)[:, None], (tile_rows, HD))
    packed = jnp.concatenate([latent[0], tag], axis=1)
    hop = lambda values, axis, by: lax.ppermute(
        values, axis, [(i, i ^ by) for i in range(row_groups if axis == "sx" else blocks)]
    )
    text_parts = [text_local] + [hop(text_local, "sx", k) for k in range(1, row_groups)]
    text_grad_parts = [text_grad[0]] + [hop(text_grad[0], "sx", k) for k in range(1, row_groups)]
    side = spread_over(packed, axes, devices)

    gain = norm_gain.reshape(1, width)
    small = jax.ShapeDtypeStruct
    square = small((down_chan, down_chan), BF16)
    proj, proj_t, mapped, u, gram, z, conv_t = small_products(
        head, w_query, w_key, w_value, w_out, gain, w_down_proj, w_up_proj, w_down_conv
    )

    def to_heads(values):
        return lax.all_to_all(jnp.repeat(values, repeat, axis=0) if repeat > 1 else values, "sy", 0, 0)

    text_here = text_heads(head, text_parts, gain, w_query, w_key, w_value, proj)
    text = to_heads(text_here).reshape(text_total, 3 * HD)

    side = side.reshape(blocks, row_groups, tile_rows, -1)
    lat_t = side[..., : tile_cols * lat_chan].reshape(total, lat_chan).T.astype(F32)
    offsets = side[:, 0, 0, tile_cols * lat_chan].astype(jnp.int32)
    block_ids = jnp.arange(blocks, dtype=jnp.int32)
    thr = block_ids * text_block + offsets
    ids = np.arange(length, dtype=np.int32)
    cell = np.stack([ids // tile_cols, ids % tile_cols])
    at = np.arange(blocks)[:, None]
    steps = rope_tables(ids)
    steps_t = np.ascontiguousarray(np.swapaxes(steps, 1, 2)[:, HD // 2 :])
    starts = rope_tables((at * block_len + np.arange(text_block + 1)).reshape(-1))
    near = (at * block_len + np.arange(text_block)).reshape(-1)
    near, far = rope_tables(near), rope_tables(near + length)

    chunk = lambda kind, rows=length, cols=HD: small((blocks, rows, cols), kind)
    text_kind = small((text_total, HD), BF16)
    text_flip = small((HD, text_total), BF16)
    side_len = max(length, text_total)
    pre_down, act_t, patch_t, q_img, qt, k_img, kt, v_img, vt = image_rows(
        (high, tile_cols, width, 1), thr, lat_t, cell, conv_t, proj_t, mapped, gram, starts, steps, steps_t, text_here
    )
    part, q_txt, qt_txt, k_txt, kt_txt, mix_t, mix_txt_t, mix_txt, lse, lse_txt = call(
        attend_kernel, head,
        [(thr, "smem"), (text, None), (near, None), (far, None), (qt, None), (k_img, None), (vt, None), (u, None)],
        [chunk(BF16, length, up_chan), text_kind, text_flip, text_kind, text_flip, chunk(BF16, HD, length),
         text_flip, text_kind, small((blocks, 1, length), F32), small((1, text_total), F32)],
        [pltpu.VMEM((blocks + 3, side_len, side_len), F32), pltpu.VMEM((HD, text_total), BF16),
         pltpu.VMEM((2, HD, length), F32), pltpu.VMEM((2, 1, length), F32), pltpu.VMEM((2, 1, length), F32)],
        flops=6_000_000_000,
    )

    own_rows = tile_rows * tile_cols
    part = part if repeat == 1 else part * jnp.asarray(copies, BF16)
    parts = lax.all_to_all(part.reshape(devices, own_rows, up_chan), axes, 0, 0)
    text_back = text_grad_heads(head, text_grad_parts, w_out, mix_txt, repeat, part)
    text_back = [text_back[0]] + [hop(text_back[k], "sy", k) for k in range(1, blocks)]
    grad_copies, prediction, grad_out_t = call(
        up_kernel, head,
        [(parts, None), (pre_down.reshape(devices, own_rows, down_chan), "mine"), (z, None), (w_up_out, None),
         (pred_grad[0].reshape(own_rows, lat_chan), None)],
        [small((devices, own_rows, up_chan), BF16), small((own_rows, lat_chan), BF16), small((lat_chan, up_chan), F32)],
        flops=2_000_000_000,
        after=text_back[:1],
        room=SMALL_BYTES,
    )
    grad_pre = lax.all_to_all(grad_copies, axes, 0, 0).reshape(blocks, length, up_chan)

    mixed = text_out_parts(head, text_back, w_out, repeat, row_groups)
    mixed = [mixed[0]] + [hop(mixed[k], "sx", k) for k in range(1, row_groups)]
    text_out = (text_local.astype(F32) + sum(m.astype(F32) for m in mixed)).astype(BF16)

    pairs = blocks // 2
    own_part = width // devices
    few = -(-(taps + lat_chan) // (16 * devices)) * 16
    piece = lambda rows: small((row_groups, pairs, rows, HD), BF16)
    lump = lambda rows: small((pairs, rows, HD), BF16)
    flat = lambda rows: small((rows, HD), BF16)
    vmem = pltpu.VMEM
    lay = lambda rows: vmem((2, row_groups, pairs, rows, HD), BF16)

    def core_sum(keep, send, rows):
        return plain(add_core_kernel, [keep, hop(send, "sy", 1)], [lump(rows)] * row_groups)

    def sx_sum(sums, rows, after=()):
        sums = [sums[0]] + [hop(sums[k], "sx", k) for k in range(1, row_groups)]
        return plain(lambda *refs: add_sx_kernel(row_groups, *refs), sums, [flat(rows)] * pairs, after)

    def z_sum(sums, rows, after=()):
        sums = [sums[0]] + [hop(sums[m], "sy", 2 * m) for m in range(1, pairs)]
        return plain(add_kernel, sums, [flat(rows)], after)[0]

    def spread_z(mine):
        return jnp.stack([mine] + [hop(mine, "sy", 2 * m) for m in range(1, pairs)])

    def spread_sx(mine):
        near = [mine] + [hop(mine, "sx", k) for k in range(1, row_groups)]
        return near + [hop(values, "sy", 1) for values in near]

    wide = vmem((blocks, length, HD), F32)
    rows = 2 * own_part + few
    keep, send = call(
        lambda *refs: backward_kernel(share, copies, 1, *refs), head,
        [(thr, "smem")] + [(a, None) for a in (
            grad_pre, q_img, qt, k_img, kt, v_img, q_txt, qt_txt, k_txt, kt_txt, text, mix_t, mix_txt_t, lse, lse_txt,
            u, proj, gram, z, gain, starts, steps, grad_out_t, *text_back)]
        + [(a, "any") for a in (
            pre_down, act_t, patch_t, w_query, w_key, w_value, w_out, w_up_proj, w_down_proj)],
        [piece(rows)] * 2,
        [wide, wide, wide, vmem((2, length, HD), BF16), vmem((2, HD, length), BF16), vmem((2, HD, length), F32),
         vmem((text_total, HD), BF16), vmem((HD, up_chan), F32), vmem((devices * few, HD), F32)]
        + [vmem(a.shape, a.dtype) for a in (pre_down, act_t, patch_t)]
        + [vmem((width, HD), BF16)] * 3
        + [vmem((HD, width), BF16), vmem(w_up_proj.shape, BF16), vmem(w_down_proj.shape, BF16), lay(rows),
           pltpu.SemaphoreType.DMA((9,))],
        flops=30_000_000_000,
        after=[text_out],
        out_kind="any",
    )
    mine = spread_z(z_sum(sx_sum(core_sum(keep, send, rows), rows), rows))
    grad_conv, grad_down, grad_up, grad_out_t = call(
        lambda *refs: unpack_kernel(row_groups, pairs, own_part, *refs), head,
        [(a, None) for a in spread_sx(mine)],
        [small((taps, down_chan), F32), small((down_chan, width), F32), small((width, up_chan), F32),
         small((lat_chan, up_chan), F32)],
        [vmem((devices * few, HD), F32)],
        room=2 * SMALL_BYTES,
    )
    return (
        prediction.reshape(1, tile_rows, tile_cols * lat_chan),
        text_out[None],
        grad_conv,
        grad_down,
        grad_up,
        grad_out_t.T,
    )


def solution(mesh):
    placed = (
        P("sy", "sx", None),
        P("sy", "sx", None),
        P("sy"),
        P(),
        P(None, "sx"),
        P(None, "sx"),
        P(None, "sx"),
        P("sx", None),
        P(),
        P(),
        P(),
        P(),
        P("sy", "sx", None),
        P("sy", "sx", None),
    )
    return jax.shard_map(
        shards,
        mesh=mesh,
        in_specs=placed,
        out_specs=(P("sy", "sx", None), P("sy", "sx", None), P(), P(), P(), P()),
        check_vma=False,
    )
```

time: 826 us -> 235 us (0.28)
  waiting for transfers between devices: 411 us -> 52.5 us
  matrix products: 140 us -> 0 us
  local copies, waits for them, and re-layouts: 130 us -> 37.3 us
  Pallas kernels: 0 us -> 82.5 us
  other arithmetic: 69.9 us -> 0.98 us
  starting transfers between devices: 7.83 us -> 58.7 us
  blocking collectives: 39.8 us -> 0 us
  between operations: 15.3 us -> 1.83 us
  loops' own time: 8.4 us -> 0 us
    all_gather x3 -> x0, waiting for transfers between devices: 142 us -> none  [the longest x1 89.4 us: shards(): every_key = lax.all_gather(keys_values, 'sy', axis=0, tiled=True)]
    dot_general x77 -> x0, matrix products: 140 us -> none  [the longest x9 29.5 us: mix_keys(): jnp.einsum('hqk,khd->qhd', probs.astype(jnp.bfloat16), value_heads, prefe...]
    psum x1 -> x0, waiting for transfers between devices: 103 us -> none  [shards(): lax.psum((grad_down_conv, grad_down_proj, grad_up_proj, grad_up_out), ('s...]
    reduce_scatter x1 -> x0, waiting for transfers between devices: 97.7 us -> none  [shards(): lax.psum_scatter(grads_term.astype(wide_type).astype(jnp.bfloat16), 'sy',...]
    pallas_call x0 -> x12, Pallas kernels: none -> 82.5 us  [the longest x4 44.5 us: call(): pl.pallas_call(lambda head_ref, *refs: kernel(head_ref, *refs[skip:]), ou...]
    unnamed x9 -> x0, waiting for transfers between devices: 68.4 us -> none
    ppermute x2 -> x33, waiting for transfers between devices: 0.01 us -> 52.5 us  [shards(): lax.ppermute(values, axis, [(i, i ^ by) for i in range(row_groups if axis...]
    psum x1 -> x0, blocking collectives: 39.8 us -> none  [shards(): lax.psum((grad_down_conv, grad_down_proj, grad_up_proj, grad_up_out), ('s...]
  transfers between devices with their start and end apart: 9 -> 37, of which waited for: 7 -> 19; matrix products, arithmetic and copies ran while one was open for 4% -> 2% of each run, Pallas kernels for 0% -> 17%
where the time goes in v1:
time: 235 us; the launch traced here: 234 us
  Pallas kernels  82.5 us (35%)
  starting transfers between devices  58.7 us (25%)
  waiting for transfers between devices  52.5 us (22%)
  local copies, waits for them, and re-layouts  37.3 us (16%)
    ppermute x33, waiting for transfers between devices, shards(): lax.ppermute(values, axis, [(i, i ^ by) for i in range(row_groups if axis...  52.5 us
    pallas_call x4, Pallas kernels, call(): pl.pallas_call(lambda head_ref, *refs: kernel(head_ref, *refs[skip:]), ou...  44.5 us
    ppermute x33, starting transfers between devices, shards(): lax.ppermute(values, axis, [(i, i ^ by) for i in range(row_groups if axis...  37.1 us
    unnamed x119, local copies, waits for them, and re-layouts  33.7 us
    pallas_call x1, Pallas kernels, text_heads(): pl.pallas_call(lambda *refs: text_kernel(len(parts), *refs), out_shape=ja...  13.8 us
    pallas_call x1, Pallas kernels, text_grad_heads(): pl.pallas_call(lambda *refs: text_grad_kernel(len(parts), *refs), out_sha...  9.77 us
    pallas_call x1, Pallas kernels, image_rows(): pl.pallas_call(lambda *refs: image_kernel(*sizes, *refs), out_shape=[jax....  6.41 us
    all_to_all x1, starting transfers between devices, spread_over(): lax.all_to_all(jnp.broadcast_to(values[None], (count,) + values.shape), a...  6.25 us
  transfers between devices with their start and end apart: 37, of which 19 were waited for; matrix products, arithmetic and copies ran while one was open for 2% of the time, Pallas kernels for 17%

profile of v1, /device:TPU:0, one launch (start us, length us, event | category | flops | bytes accessed | tf_op | source)
XLA Modules:
  0.0 233.8 jit_solution(10131524059214343173)
XLA Ops:
  0.6 4.0 %collective-permute-start.5 = (bf16[8,4096]{1,0:T(8,128)(2,1)}, bf16[8,4096]{1,0:T(8,128)(2,1)S(1)}, u32[]{:S(2)}, u32[]{:S(2)}) collective-permute-start(bf16[8,4096]{1,0:T(8,128)(2,1)} %bitcast.29), channel_id=1, source_target_pairs={{0,24},{8,16},{16,8},{24,0},{1,25},{9,17},{17,9},{25,1},{2,26},{10... | collective-permute-start | bytes 196616 | tf_op jit(solution)/shard_map/ppermute | solution.py:714
  7.3 6.2 %all-to-all-start = ((bf16[32,4,640]{2,1,0:T(4,128)(2,1)}), bf16[32,4,640]{2,1,0:T(4,128)(2,1)S(1)}, u32[]{:S(2)}, u32[]{:S(2)}) async-start(bf16[32,4,640]{2,1,0:T(4,128)(2,1)} %broadcast_in_dim.7), calls=%async_computation | async-start | bytes 327680 | tf_op jit(solution)/shard_map/all_to_all | solution.py:710
  14.4 3.4 %copy-done = bf16[1024,4096]{1,0:T(8,128)(2,1)S(1)} copy-done((bf16[1024,4096]{1,0:T(8,128)(2,1)S(1)}, bf16[1024,4096]{1,0:T(8,128)(2,1)}, u32[]{:S(2)}) %copy-start) | copy-done | bytes 8388632
  17.8 3.4 %copy-done.2 = bf16[4096,1024]{1,0:T(8,128)(2,1)S(1)} copy-done((bf16[4096,1024]{1,0:T(8,128)(2,1)S(1)}, bf16[4096,1024]{1,0:T(8,128)(2,1)}, u32[]{:S(2)}) %copy-start.2) | copy-done | bytes 8388632
  21.2 3.4 %copy-done.3 = bf16[4096,1024]{1,0:T(8,128)(2,1)S(1)} copy-done((bf16[4096,1024]{1,0:T(8,128)(2,1)S(1)}, bf16[4096,1024]{1,0:T(8,128)(2,1)}, u32[]{:S(2)}) %copy-start.3) | copy-done | bytes 8388632
  24.6 3.4 %copy-done.4 = bf16[4096,1024]{1,0:T(8,128)(2,1)S(1)} copy-done((bf16[4096,1024]{1,0:T(8,128)(2,1)S(1)}, bf16[4096,1024]{1,0:T(8,128)(2,1)}, u32[]{:S(2)}) %copy-start.4) | copy-done | bytes 8388632
  27.9 1.2 copy-done.6
  29.2 1.2 copy-done.7
  30.4 0.9 copy-done.11
  31.3 4.3 %shard_map.235 = (bf16[128,384]{1,0:T(8,128)(2,1)S(1)}, bf16[384,128]{1,0:T(8,128)(2,1)S(1)}, bf16[128,640]{1,0:T(8,128)(2,1)S(1)}, bf16[128,128]{1,0:T(8,128)(2...) custom-call(s32[6]{0:T(128)S(1)} %stack.39.head.refs_0_.head_ref, ...), custom_call_target="tpu_custom_call" | custom-call | flops 4000000000 | bytes 6291456 | tf_op jit(solution)/shard_map/pallas_call | solution.py:129
  37.5 13.8 %shard_map.236.refs_10_ = bf16[8,32,384]{2,1,0:T(8,128)(2,1)} custom-call(s32[6]{0:T(128)} %copy-done.12, bf16[8,4096]{1,0:T(8,128)(2,1)} %bitcast.32, bf16[8,4096]{1,0:T(8,128)(2,1)} %copy-done.48, bf16[8,4096]{1,0:T(8,128)(2,1)} %copy-done.47, bf16[8,4096]{1,0:T(8,128)(2,1)} %copy-done.46, bf16[1,4096]{1,0:T(2,128)(2,1)} %copy-done.9, ...), custom_call_target="tpu_custom_call" | custom-call | flops 805306368 | bytes 25165824 | tf_op jit(solution)/shard_map/pallas_call | solution.py:191
  51.3 5.0 %all-to-all-start.1 = ((bf16[8,32,384]{2,1,0:T(8,128)(2,1)}), bf16[8,32,384]{2,1,0:T(8,128)(2,1)S(1)}, u32[]{:S(2)}, u32[]{:S(2)}) async-start(bf16[8,32,384]{2,1,0:T(8,128)(2,1)} %shard_map.236.refs_10_), calls=%async_computation.1 | async-start | bytes 393216 | tf_op jit(solution)/shard_map/all_to_all | solution.py:729
  57.3 6.4 %shard_map.237 = (f32[8,256,128]{2,1,0:T(8,128)S(1)}, bf16[8,128,256]{2,1,0:T(8,128)(2,1)S(1)}, bf16[8,288,256]{2,1,0:T(8,128)(2,1)S(1)}, bf16[8,256,128]{2,1,0:...) custom-call(s32[8]{0:T(128)S(1)} %multiply_add_fusion.refs_0_.refs_1, ...), custom_call_target="tpu_custom_call" | custom-call | flops 8000000000 | bytes 8000000 | tf_op jit(solution)/shard_map/pallas_call | solution.py:364
  63.8 1.0 copy-done.33
  64.8 0.8 copy-done.34
  65.6 0.8 copy-done.35
  66.4 0.8 copy-done.36
  67.1 0.8 copy-done.37
  68.0 0.8 copy-done.38
  68.8 0.8 copy-done.39
  69.6 0.8 copy-done.40
  71.1 11.3 %shard_map.238 = (bf16[8,256,128]{2,1,0:T(8,128)(2,1)}, bf16[256,128]{1,0:T(8,128)(2,1)}, bf16[128,256]{1,0:T(8,128)(2,1)}, bf16[256,128]{1,0:T(8,128)(2,1)}, bf...) custom-call(s32[6]{0:T(128)} %copy-done.12, ...), custom_call_target="tpu_custom_call" | custom-call | flops 6000000000 | bytes 3777568 | tf_op jit(solution)/shard_map/pallas_call | solution.py:72
  82.4 6.0 %all-to-all-start.2 = ((bf16[32,64,128]{2,1,0:T(8,128)(2,1)}), bf16[32,64,128]{2,1,0:T(8,128)(2,1)S(1)}, u32[]{:S(2)}, u32[]{:S(2)}) async-start(bf16[32,64,128]{2,1,0:T(8,128)(2,1)} %bitcast.25), calls=%async_computation.2 | async-start | bytes 1048576 | tf_op jit(solution)/shard_map/all_to_all | solution.py:767
  88.5 2.7 %collective-permute-start.2 = (bf16[8,4096]{1,0:T(8,128)(2,1)S(1)}, bf16[8,4096]{1,0:T(8,128)(2,1)S(1)}, u32[]{:S(2)}, u32[]{:S(2)}) collective-permute-start(bf16[8,4096]{1,0:T(8,128)(2,1)S(1)} %bitcast.39), channel_id=1, source_target_pairs={{0,24},{8,16},{16,8},{24,0},{1,25},{9,17},{17,9},{25,1},{2,26},{10... | collective-permute-start | bytes 196616 | tf_op jit(solution)/shard_map/ppermute | solution.py:714
  92.3 5.7 %collective-permute-done.2.refs_4_ = bf16[8,4096]{1,0:T(8,128)(2,1)S(1)} collective-permute-done((bf16[8,4096]{1,0:T(8,128)(2,1)S(1)}, bf16[8,4096]{1,0:T(8,128)(2,1)S(1)}, u32[]{:S(2)}, u32[]{:S(2)}) %collective-permute-start.2) | collective-permute-done | bytes 65568 | tf_op jit(solution)/shard_map/ppermute | solution.py:714
  98.0 1.0 collective-permute-done.1.refs_3_
  99.6 9.8 %shard_map.239 = (bf16[32,256]{1,0:T(8,128)(2,1)}, bf16[32,256]{1,0:T(8,128)(2,1)}, bf16[32,256]{1,0:T(8,128)(2,1)}, bf16[32,256]{1,0:T(8,128)(2,1)}, bf16[32,25...) custom-call(s32[6]{0:T(128)} %copy-done.12, ...), custom_call_target="tpu_custom_call" | custom-call | flops 268435456 | bytes 8388608 | tf_op jit(solution)/shard_map/pallas_call | solution.py:232
  109.5 1.2 collective-permute-start.7
  111.4 1.6 shard_map.240
  113.6 4.3 %all-to-all-start.3 = ((bf16[32,64,128]{2,1,0:T(8,128)(2,1)}), bf16[32,64,128]{2,1,0:T(8,128)(2,1)S(1)}, u32[]{:S(2)}, u32[]{:S(2)}) async-start(bf16[32,64,128]{2,1,0:T(8,128)(2,1)} %get-tuple-element.87), calls=%async_computation.3 | async-start | bytes 1048576 | tf_op jit(solution)/shard_map/all_to_all | solution.py:779
  118.0 1.4 collective-permute-start.8
  119.4 2.4 %collective-permute-start.9 = (bf16[32,256]{1,0:T(8,128)(2,1)S(1)}, bf16[32,256]{1,0:T(8,128)(2,1)S(1)}, u32[]{:S(2)}, u32[]{:S(2)}) collective-permute-start(bf16[32,256]{1,0:T(8,128)(2,1)S(1)} %copy-done.57), channel_id=1, source_target_pairs={{0,4},{1,5},{2,6},{3,7},{4,0},{5,1},{6,2},{7,3},{8,12},{9,13},{10,... | collective-permute-start | bytes 49160 | tf_op jit(solution)/shard_map/ppermute | solution.py:714
  122.0 2.4 %collective-permute-start.11 = (bf16[32,256]{1,0:T(8,128)(2,1)S(1)}, bf16[32,256]{1,0:T(8,128)(2,1)S(1)}, u32[]{:S(2)}, u32[]{:S(2)}) collective-permute-start(bf16[32,256]{1,0:T(8,128)(2,1)S(1)} %copy-done.55), channel_id=1, source_target_pairs={{0,6},{1,7},{2,4},{3,5},{4,2},{5,3},{6,0},{7,1},{8,14},{9,15},{10,... | collective-permute-start | bytes 49160 | tf_op jit(solution)/shard_map/ppermute | solution.py:714
  124.5 1.3 collective-permute-start.12
  125.7 2.0 collective-permute-done.8.refs_4_.refs_28_
  127.7 7.3 %collective-permute-done.9.refs_5_.refs_29_ = bf16[32,256]{1,0:T(8,128)(2,1)S(1)} collective-permute-done((bf16[32,256]{1,0:T(8,128)(2,1)S(1)}, bf16[32,256]{1,0:T(8,128)(2,1)S(1)}, u32[]{:S(2)}, u32[]{:S(2)}) %collective-permute-start.9) | collective-permute-done | bytes 16416 | tf_op jit(solution)/shard_map/ppermute | solution.py:714
  135.1 3.4 %copy-done.1 = bf16[1024,4096]{1,0:T(8,128)(2,1)S(1)} copy-done((bf16[1024,4096]{1,0:T(8,128)(2,1)S(1)}, bf16[1024,4096]{1,0:T(8,128)(2,1)}, u32[]{:S(2)}) %copy-start.1) | copy-done | bytes 8388632
  138.5 3.4 %shard_map.241 = (bf16[8,4096]{1,0:T(8,128)(2,1)S(1)}, bf16[8,4096]{1,0:T(8,128)(2,1)S(1)}, bf16[8,4096]{1,0:T(8,128)(2,1)S(1)}, bf16[8,4096]{1,0:T(8,128)(2,1)S(1)}) custom-call(s32[6]{0:T(128)S(1)} %copy-done.13, bf16[32,256]{1,0:T(8,128)(2,1)S(1)} %copy-done.16, bf16[32,256]{1,0:T(8,128)(2,1)S(1)} %collective-permute-done.6.refs_2_.refs_26_, ...), custom_call_target="tpu_custom_call" | custom-call | flops 268435456 | bytes 8388608 | tf_op jit(solution)/shard_map/pallas_call | solution.py:273
  141.9 1.5 collective-permute-start.13
  143.4 1.5 collective-permute-start.14
  145.5 0.8 collective-permute-done.13
  146.3 1.4 collective-permute-done.14
  147.7 2.4 %collective-permute-done.15 = bf16[8,4096]{1,0:T(8,128)(2,1)S(1)} collective-permute-done((bf16[8,4096]{1,0:T(8,128)(2,1)S(1)}, bf16[8,4096]{1,0:T(8,128)(2,1)S(1)}, u32[]{:S(2)}, u32[]{:S(2)}) %collective-permute-start.15) | collective-permute-done | bytes 65568 | tf_op jit(solution)/shard_map/ppermute | solution.py:714
  150.8 0.8 copy-done.42
  151.6 28.7 %shard_map.242 = (bf16[4,4,272,128]{3,2,1,0:T(8,128)(2,1)}, bf16[4,4,272,128]{3,2,1,0:T(8,128)(2,1)}) custom-call(s32[6]{0:T(128)} %copy-done.12, bf16[8,4096]{1,0:T(8,128)(2,1)} %add_convert_fusion.refs_0_, s32[8]{0:T(128)} %copy-done.31, bf16[8,256,128]{2,1,0:T(8,128)(2,1)} %bitcast.28, bf16[8,256,128]{2,1,0:T(8,128)(2,1)} %copy-done.38, ...), custom_call_target="tpu_custom_call" | custom-call | flops 30000001024 | bytes 45786144 | tf_op jit(solution)/shard_map/pallas_call | solution.py:72
  180.4 3.0 %collective-permute-done.16.refs_1_ = bf16[4,4,272,128]{3,2,1,0:T(8,128)(2,1)S(1)} collective-permute-done((bf16[4,4,272,128]{3,2,1,0:T(8,128)(2,1)}, bf16[4,4,272,128]{3,2,1,0:T(8,128)(2,1)S(1)}, u32[]{:S(2)}, u32[]{:S(2)}) %collective-permute-start.16) | collective-permute-done | bytes 1114144 | tf_op jit(solution)/shard_map/ppermute | solution.py:714
  183.3 1.2 copy-done.5
  186.0 2.4 %collective-permute-start.19 = (bf16[4,272,128]{2,1,0:T(8,128)(2,1)S(1)}, bf16[4,272,128]{2,1,0:T(8,128)(2,1)S(1)}, u32[]{:S(2)}, u32[]{:S(2)}) collective-permute-start(bf16[4,272,128]{2,1,0:T(8,128)(2,1)S(1)} %get-tuple-element.107), channel_id=1, source_target_pairs={{0,24},{8,16},{16,8},{24,0},{1,25},{9,17},{17,9},{25,1},{2,26},{10... | collective-permute-start | bytes 835592 | tf_op jit(solution)/shard_map/ppermute | solution.py:714
  188.4 6.0 %collective-permute-done.17.refs_1_ = bf16[4,272,128]{2,1,0:T(8,128)(2,1)S(1)} collective-permute-done((bf16[4,272,128]{2,1,0:T(8,128)(2,1)S(1)}, bf16[4,272,128]{2,1,0:T(8,128)(2,1)S(1)}, u32[]{:S(2)}, u32[]{:S(2)}) %collective-permute-start.17) | collective-permute-done | bytes 278560 | tf_op jit(solution)/shard_map/ppermute | solution.py:714
  194.4 5.4 %collective-permute-done.18.refs_2_ = bf16[4,272,128]{2,1,0:T(8,128)(2,1)S(1)} collective-permute-done((bf16[4,272,128]{2,1,0:T(8,128)(2,1)S(1)}, bf16[4,272,128]{2,1,0:T(8,128)(2,1)S(1)}, u32[]{:S(2)}, u32[]{:S(2)}) %collective-permute-start.18) | collective-permute-done | bytes 278560 | tf_op jit(solution)/shard_map/ppermute | solution.py:714
  200.0 1.0 collective-permute-start.20
  201.0 0.8 collective-permute-start.21
  201.8 2.7 %collective-permute-start.22 = (bf16[272,128]{1,0:T(8,128)(2,1)S(1)}, bf16[272,128]{1,0:T(8,128)(2,1)S(1)}, u32[]{:S(2)}, u32[]{:S(2)}) collective-permute-start(bf16[272,128]{1,0:T(8,128)(2,1)S(1)} %get-tuple-element.111), channel_id=1, source_target_pairs={{0,6},{1,7},{2,4},{3,5},{4,2},{5,3},{6,0},{7,1},{8,14},{9,15},{10,... | collective-permute-start | bytes 208904 | tf_op jit(solution)/shard_map/ppermute | solution.py:714
  204.7 3.7 %collective-permute-done.21.refs_2_ = bf16[272,128]{1,0:T(8,128)(2,1)S(1)} collective-permute-done((bf16[272,128]{1,0:T(8,128)(2,1)S(1)}, bf16[272,128]{1,0:T(8,128)(2,1)S(1)}, u32[]{:S(2)}, u32[]{:S(2)}) %collective-permute-start.21) | collective-permute-done | bytes 69664 | tf_op jit(solution)/shard_map/ppermute | solution.py:714
  208.5 2.2 collective-permute-start.25
  211.3 1.6 collective-permute-start.23
  213.0 1.8 collective-permute-done.25
  214.8 1.6 collective-permute-done.24
  216.5 1.5 collective-permute-start.28
  218.0 1.2 collective-permute-start.27
  219.2 0.8 collective-permute-start.26
  220.0 6.2 %collective-permute-done.28.refs_3_ = bf16[4,272,128]{2,1,0:T(8,128)(2,1)S(1)} collective-permute-done((bf16[4,272,128]{2,1,0:T(8,128)(2,1)S(1)}, bf16[4,272,128]{2,1,0:T(8,128)(2,1)S(1)}, u32[]{:S(2)}, u32[]{:S(2)}) %collective-permute-start.28) | collective-permute-done | bytes 278560 | tf_op jit(solution)/shard_map/ppermute | solution.py:714
  226.2 2.8 %collective-permute-done.27.refs_2_ = bf16[4,272,128]{2,1,0:T(8,128)(2,1)S(1)} collective-permute-done((bf16[4,272,128]{2,1,0:T(8,128)(2,1)S(1)}, bf16[4,272,128]{2,1,0:T(8,128)(2,1)S(1)}, u32[]{:S(2)}, u32[]{:S(2)}) %collective-permute-start.27) | collective-permute-done | bytes 278560 | tf_op jit(solution)/shard_map/ppermute | solution.py:714
  231.0 2.8 %shard_map.246 = (f32[288,128]{1,0:T(8,128)}, f32[128,4096]{1,0:T(8,128)}, f32[4096,128]{1,0:T(8,128)}, f32[32,128]{1,0:T(8,128)}) custom-call(s32[6]{0:T(128)S(1)} %copy-done.14, bf16[4,272,128]{2,1,0:T(8,128)(2,1)S(1)} %pad_maximum_fusion.refs_0_, bf16[4,272,128]{2,1,0:T(8,128)(2,1)S(1)} %collective-permute-done.26.refs_1_, ...), custom_call_target="tpu_custom_call" | custom-call | bytes 6586368 | tf_op jit(solution)/shard_map/pallas_call | solution.py:72
  (154 shorter events, 15.5 us)
Async XLA Ops:
  0.6 36.2 %collective-permute-start.5 = (bf16[8,4096]{1,0:T(8,128)(2,1)}, bf16[8,4096]{1,0:T(8,128)(2,1)S(1)}, u32[]{:S(2)}, u32[]{:S(2)}) collective-permute-start(bf16[8,4096]{1,0:T(8,128)(2,1)} %bitcast.29), channel_id=1, source_target_pairs={{0,24},{8,16},{16,8},{24,0},{1,25},{9,17},{17,9},{25,1},{2,26},{10... | collective-permute-start | bytes 196616 | tf_op jit(solution)/shard_map/ppermute | solution.py:714
  4.6 32.2 %collective-permute-start.4 = (bf16[8,4096]{1,0:T(8,128)(2,1)}, bf16[8,4096]{1,0:T(8,128)(2,1)S(1)}, u32[]{:S(2)}, u32[]{:S(2)}) collective-permute-start(bf16[8,4096]{1,0:T(8,128)(2,1)} %bitcast.30), channel_id=1, source_target_pairs={{0,16},{8,24},{16,0},{24,8},{1,17},{9,25},{17,1},{25,9},{2,18},{10... | collective-permute-start | bytes 196616 | tf_op jit(solution)/shard_map/ppermute | solution.py:714
  5.1 31.7 %collective-permute-start.3 = (bf16[8,4096]{1,0:T(8,128)(2,1)}, bf16[8,4096]{1,0:T(8,128)(2,1)S(1)}, u32[]{:S(2)}, u32[]{:S(2)}) collective-permute-start(bf16[8,4096]{1,0:T(8,128)(2,1)} %bitcast.31), channel_id=1, source_target_pairs={{0,8},{8,0},{16,24},{24,16},{1,9},{9,1},{17,25},{25,17},{2,10},{10... | collective-permute-start | bytes 196616 | tf_op jit(solution)/shard_map/ppermute | solution.py:714
  7.3 44.0 %all-to-all-start = ((bf16[32,4,640]{2,1,0:T(4,128)(2,1)}), bf16[32,4,640]{2,1,0:T(4,128)(2,1)S(1)}, u32[]{:S(2)}, u32[]{:S(2)}) async-start(bf16[32,4,640]{2,1,0:T(4,128)(2,1)} %broadcast_in_dim.7), calls=%async_computation | async-start | bytes 327680 | tf_op jit(solution)/shard_map/all_to_all | solution.py:710
  14.3 21.3 %copy-start.9 = (bf16[1,4096]{1,0:T(2,128)(2,1)}, bf16[1,4096]{1,0:T(2,128)(2,1)S(1)}, u32[]{:S(2)}) copy-start(bf16[1,4096]{1,0:T(2,128)(2,1)S(1)} %reshape.41.gain.refs_5_.refs_21_) | copy-start | bytes 24580
  36.8 20.5 %copy-start.25 = (bf16[128,128]{1,0:T(8,128)(2,1)}, bf16[128,128]{1,0:T(8,128)(2,1)S(1)}, u32[]{:S(2)}) copy-start(bf16[128,128]{1,0:T(8,128)(2,1)S(1)} %get-tuple-element.65.refs_6_.refs_19_) | copy-start | bytes 98308
  36.8 73.9 %copy-start.26 = (bf16[128,128]{1,0:T(8,128)(2,1)}, bf16[128,128]{1,0:T(8,128)(2,1)S(1)}, u32[]{:S(2)}) copy-start(bf16[128,128]{1,0:T(8,128)(2,1)S(1)} %get-tuple-element.74.refs_3_.refs_20_) | copy-start | bytes 98308
  51.3 6.0 %copy-start.28 = (f32[2,264,128]{2,1,0:T(8,128)S(1)}, f32[2,264,128]{2,1,0:T(8,128)}, u32[]{:S(2)}) copy-start(f32[2,264,128]{2,1,0:T(8,128)} %constant.58.clone.refs_7_.refs_22_) | copy-start | bytes 811012
  51.3 6.0 %copy-start.29 = (f32[2,256,128]{2,1,0:T(8,128)S(1)}, f32[2,256,128]{2,1,0:T(8,128)}, u32[]{:S(2)}) copy-start(f32[2,256,128]{2,1,0:T(8,128)} %constant.59.clone.refs_8_.refs_23_) | copy-start | bytes 786436
  51.3 6.0 %copy-start.30 = (f32[2,64,256]{2,1,0:T(8,128)S(1)}, f32[2,64,256]{2,1,0:T(8,128)}, u32[]{:S(2)}) copy-start(f32[2,64,256]{2,1,0:T(8,128)} %constant.60.clone.refs_9_) | copy-start | bytes 393220
  51.3 6.0 %copy-start.32 = (s32[2,256]{1,0:T(2,128)S(1)}, s32[2,256]{1,0:T(2,128)}, u32[]{:S(2)}) copy-start(s32[2,256]{1,0:T(2,128)} %constant.57.clone.refs_2_) | copy-start | bytes 6148
  51.3 19.1 %all-to-all-start.1 = ((bf16[8,32,384]{2,1,0:T(8,128)(2,1)}), bf16[8,32,384]{2,1,0:T(8,128)(2,1)S(1)}, u32[]{:S(2)}, u32[]{:S(2)}) async-start(bf16[8,32,384]{2,1,0:T(8,128)(2,1)} %shard_map.236.refs_10_), calls=%async_computation.1 | async-start | bytes 393216 | tf_op jit(solution)/shard_map/all_to_all | solution.py:729
  56.6 7.1 %copy-start.31 = (s32[8]{0:T(128)}, s32[8]{0:T(128)S(1)}, u32[]{:S(2)}) copy-start(s32[8]{0:T(128)S(1)} %multiply_add_fusion.refs_0_.refs_1_) | copy-start | bytes 100
  70.4 40.3 %copy-start.27 = (f32[8,256,128]{2,1,0:T(8,128)}, f32[8,256,128]{2,1,0:T(8,128)S(1)}, u32[]{:S(2)}) copy-start(f32[8,256,128]{2,1,0:T(8,128)S(1)} %get-tuple-element.73.refs_33_) | copy-start | bytes 3145732
  71.1 17.4 %copy-start.45 = (bf16[1,8,4096]{2,1,0:T(8,128)(2,1)S(1)}, bf16[1,8,4096]{2,1,0:T(8,128)(2,1)}, u32[]{:S(2)}) copy-start(bf16[1,8,4096]{2,1,0:T(8,128)(2,1)} %param.33) | copy-start | bytes 196612
  71.1 21.0 %copy-start.53 = (bf16[1,4,512]{2,1,0:T(4,128)(2,1)S(1)}, bf16[1,4,512]{2,1,0:T(4,128)(2,1)}, u32[]{:S(2)}) copy-start(bf16[1,4,512]{2,1,0:T(4,128)(2,1)} %param.32) | copy-start | bytes 12292
  71.1 21.0 %copy-start.52 = (bf16[128,32]{0,1:T(8,128)(2,1)S(1)}, bf16[128,32]{0,1:T(8,128)(2,1)}, u32[]{:S(2)}) copy-start(bf16[128,32]{0,1:T(8,128)(2,1)} %param.31) | copy-start | bytes 24580
  82.4 28.2 %all-to-all-start.2 = ((bf16[32,64,128]{2,1,0:T(8,128)(2,1)}), bf16[32,64,128]{2,1,0:T(8,128)(2,1)S(1)}, u32[]{:S(2)}, u32[]{:S(2)}) async-start(bf16[32,64,128]{2,1,0:T(8,128)(2,1)} %bitcast.25), calls=%async_computation.2 | async-start | bytes 1048576 | tf_op jit(solution)/shard_map/all_to_all | solution.py:767
  88.5 9.5 %collective-permute-start.2 = (bf16[8,4096]{1,0:T(8,128)(2,1)S(1)}, bf16[8,4096]{1,0:T(8,128)(2,1)S(1)}, u32[]{:S(2)}, u32[]{:S(2)}) collective-permute-start(bf16[8,4096]{1,0:T(8,128)(2,1)S(1)} %bitcast.39), channel_id=1, source_target_pairs={{0,24},{8,16},{16,8},{24,0},{1,25},{9,17},{17,9},{25,1},{2,26},{10... | collective-permute-start | bytes 196616 | tf_op jit(solution)/shard_map/ppermute | solution.py:714
  91.2 7.8 %collective-permute-start.1 = (bf16[8,4096]{1,0:T(8,128)(2,1)S(1)}, bf16[8,4096]{1,0:T(8,128)(2,1)S(1)}, u32[]{:S(2)}, u32[]{:S(2)}) collective-permute-start(bf16[8,4096]{1,0:T(8,128)(2,1)S(1)} %bitcast.40), channel_id=1, source_target_pairs={{0,16},{8,24},{16,0},{24,8},{1,17},{9,25},{17,1},{25,9},{2,18},{10... | collective-permute-start | bytes 196616 | tf_op jit(solution)/shard_map/ppermute | solution.py:714
  91.8 7.2 %collective-permute-start = (bf16[8,4096]{1,0:T(8,128)(2,1)S(1)}, bf16[8,4096]{1,0:T(8,128)(2,1)S(1)}, u32[]{:S(2)}, u32[]{:S(2)}) collective-permute-start(bf16[8,4096]{1,0:T(8,128)(2,1)S(1)} %bitcast.41), channel_id=1, source_target_pairs={{0,8},{8,0},{16,24},{24,16},{1,9},{9,1},{17,25},{25,17},{2,10},{10... | collective-permute-start | bytes 196616 | tf_op jit(solution)/shard_map/ppermute | solution.py:714
  99.6 11.0 %copy-start.13 = (s32[6]{0:T(128)S(1)}, s32[6]{0:T(128)}, u32[]{:S(2)}) copy-start(s32[6]{0:T(128)} %copy-done.12) | copy-start | bytes 76
  109.4 12.6 %collective-permute-start.6 = (bf16[32,256]{1,0:T(8,128)(2,1)}, bf16[32,256]{1,0:T(8,128)(2,1)S(1)}, u32[]{:S(2)}, u32[]{:S(2)}) collective-permute-start(bf16[32,256]{1,0:T(8,128)(2,1)} %get-tuple-element.76), channel_id=1, source_target_pairs={{0,1},{1,0},{2,3},{3,2},{4,5},{5,4},{6,7},{7,6},{8,9},{9,8},{10,11... | collective-permute-start | bytes 49160 | tf_op jit(solution)/shard_map/ppermute | solution.py:714
  109.5 15.0 %collective-permute-start.7 = (bf16[32,256]{1,0:T(8,128)(2,1)}, bf16[32,256]{1,0:T(8,128)(2,1)S(1)}, u32[]{:S(2)}, u32[]{:S(2)}) collective-permute-start(bf16[32,256]{1,0:T(8,128)(2,1)} %get-tuple-element.77), channel_id=1, source_target_pairs={{0,2},{1,3},{2,0},{3,1},{4,6},{5,7},{6,4},{7,5},{8,10},{9,11},{10,... | collective-permute-start | bytes 49160 | tf_op jit(solution)/shard_map/ppermute | solution.py:714
  111.4 6.6 %copy-start.58 = (bf16[32,256]{1,0:T(8,128)(2,1)S(1)}, bf16[32,256]{1,0:T(8,128)(2,1)}, u32[]{:S(2)}) copy-start(bf16[32,256]{1,0:T(8,128)(2,1)} %get-tuple-element.78) | copy-start | bytes 49156
  111.4 8.0 %copy-start.57 = (bf16[32,256]{1,0:T(8,128)(2,1)S(1)}, bf16[32,256]{1,0:T(8,128)(2,1)}, u32[]{:S(2)}) copy-start(bf16[32,256]{1,0:T(8,128)(2,1)} %get-tuple-element.79) | copy-start | bytes 49156
  111.4 10.4 %copy-start.56 = (bf16[32,256]{1,0:T(8,128)(2,1)S(1)}, bf16[32,256]{1,0:T(8,128)(2,1)}, u32[]{:S(2)}) copy-start(bf16[32,256]{1,0:T(8,128)(2,1)} %get-tuple-element.80) | copy-start | bytes 49156
  111.4 10.6 %copy-start.55 = (bf16[32,256]{1,0:T(8,128)(2,1)S(1)}, bf16[32,256]{1,0:T(8,128)(2,1)}, u32[]{:S(2)}) copy-start(bf16[32,256]{1,0:T(8,128)(2,1)} %get-tuple-element.81) | copy-start | bytes 49156
  111.4 13.0 %copy-start.54 = (bf16[32,256]{1,0:T(8,128)(2,1)S(1)}, bf16[32,256]{1,0:T(8,128)(2,1)}, u32[]{:S(2)}) copy-start(bf16[32,256]{1,0:T(8,128)(2,1)} %get-tuple-element.82) | copy-start | bytes 49156
  111.4 23.6 %copy-start.16 = (bf16[32,256]{1,0:T(8,128)(2,1)S(1)}, bf16[32,256]{1,0:T(8,128)(2,1)}, u32[]{:S(2)}) copy-start(bf16[32,256]{1,0:T(8,128)(2,1)} %get-tuple-element.72.refs_0_.refs_1_.refs_25_) | copy-start | bytes 49156
  113.6 37.1 %all-to-all-start.3 = ((bf16[32,64,128]{2,1,0:T(8,128)(2,1)}), bf16[32,64,128]{2,1,0:T(8,128)(2,1)S(1)}, u32[]{:S(2)}, u32[]{:S(2)}) async-start(bf16[32,64,128]{2,1,0:T(8,128)(2,1)} %get-tuple-element.87), calls=%async_computation.3 | async-start | bytes 1048576 | tf_op jit(solution)/shard_map/all_to_all | solution.py:779
  118.0 9.7 %collective-permute-start.8 = (bf16[32,256]{1,0:T(8,128)(2,1)S(1)}, bf16[32,256]{1,0:T(8,128)(2,1)S(1)}, u32[]{:S(2)}, u32[]{:S(2)}) collective-permute-start(bf16[32,256]{1,0:T(8,128)(2,1)S(1)} %copy-done.58), channel_id=1, source_target_pairs={{0,3},{1,2},{2,1},{3,0},{4,7},{5,6},{6,5},{7,4},{8,11},{9,10},{10,... | collective-permute-start | bytes 49160 | tf_op jit(solution)/shard_map/ppermute | solution.py:714
  119.4 15.6 %collective-permute-start.9 = (bf16[32,256]{1,0:T(8,128)(2,1)S(1)}, bf16[32,256]{1,0:T(8,128)(2,1)S(1)}, u32[]{:S(2)}, u32[]{:S(2)}) collective-permute-start(bf16[32,256]{1,0:T(8,128)(2,1)S(1)} %copy-done.57), channel_id=1, source_target_pairs={{0,4},{1,5},{2,6},{3,7},{4,0},{5,1},{6,2},{7,3},{8,12},{9,13},{10,... | collective-permute-start | bytes 49160 | tf_op jit(solution)/shard_map/ppermute | solution.py:714
  121.8 13.2 %collective-permute-start.10 = (bf16[32,256]{1,0:T(8,128)(2,1)S(1)}, bf16[32,256]{1,0:T(8,128)(2,1)S(1)}, u32[]{:S(2)}, u32[]{:S(2)}) collective-permute-start(bf16[32,256]{1,0:T(8,128)(2,1)S(1)} %copy-done.56), channel_id=1, source_target_pairs={{0,5},{1,4},{2,7},{3,6},{4,1},{5,0},{6,3},{7,2},{8,13},{9,12},{10,... | collective-permute-start | bytes 49160 | tf_op jit(solution)/shard_map/ppermute | solution.py:714
  122.0 19.8 %copy-start.17 = (bf16[32,256]{1,0:T(8,128)(2,1)}, bf16[32,256]{1,0:T(8,128)(2,1)S(1)}, u32[]{:S(2)}) copy-start(bf16[32,256]{1,0:T(8,128)(2,1)S(1)} %collective-permute-done.6.refs_2_.refs_26_) | copy-start | bytes 49156
  122.0 13.0 %collective-permute-start.11 = (bf16[32,256]{1,0:T(8,128)(2,1)S(1)}, bf16[32,256]{1,0:T(8,128)(2,1)S(1)}, u32[]{:S(2)}, u32[]{:S(2)}) collective-permute-start(bf16[32,256]{1,0:T(8,128)(2,1)S(1)} %copy-done.55), channel_id=1, source_target_pairs={{0,6},{1,7},{2,4},{3,5},{4,2},{5,3},{6,0},{7,1},{8,14},{9,15},{10,... | collective-permute-start | bytes 49160 | tf_op jit(solution)/shard_map/ppermute | solution.py:714
  124.5 17.4 %copy-start.18 = (bf16[32,256]{1,0:T(8,128)(2,1)}, bf16[32,256]{1,0:T(8,128)(2,1)S(1)}, u32[]{:S(2)}) copy-start(bf16[32,256]{1,0:T(8,128)(2,1)S(1)} %collective-permute-done.7.refs_3_.refs_27_) | copy-start | bytes 49156
  124.5 10.6 %collective-permute-start.12 = (bf16[32,256]{1,0:T(8,128)(2,1)S(1)}, bf16[32,256]{1,0:T(8,128)(2,1)S(1)}, u32[]{:S(2)}, u32[]{:S(2)}) collective-permute-start(bf16[32,256]{1,0:T(8,128)(2,1)S(1)} %copy-done.54), channel_id=1, source_target_pairs={{0,7},{1,6},{2,5},{3,4},{4,3},{5,2},{6,1},{7,0},{8,15},{9,14},{10,... | collective-permute-start | bytes 49160 | tf_op jit(solution)/shard_map/ppermute | solution.py:714
  127.7 14.1 %copy-start.19 = (bf16[32,256]{1,0:T(8,128)(2,1)}, bf16[32,256]{1,0:T(8,128)(2,1)S(1)}, u32[]{:S(2)}) copy-start(bf16[32,256]{1,0:T(8,128)(2,1)S(1)} %collective-permute-done.8.refs_4_.refs_28_) | copy-start | bytes 49156
  135.0 6.8 %copy-start.20 = (bf16[32,256]{1,0:T(8,128)(2,1)}, bf16[32,256]{1,0:T(8,128)(2,1)S(1)}, u32[]{:S(2)}) copy-start(bf16[32,256]{1,0:T(8,128)(2,1)S(1)} %collective-permute-done.9.refs_5_.refs_29_) | copy-start | bytes 49156
  135.0 6.8 %copy-start.21 = (bf16[32,256]{1,0:T(8,128)(2,1)}, bf16[32,256]{1,0:T(8,128)(2,1)S(1)}, u32[]{:S(2)}) copy-start(bf16[32,256]{1,0:T(8,128)(2,1)S(1)} %collective-permute-done.10.refs_6_.refs_30_) | copy-start | bytes 49156
  135.0 6.9 %copy-start.22 = (bf16[32,256]{1,0:T(8,128)(2,1)}, bf16[32,256]{1,0:T(8,128)(2,1)S(1)}, u32[]{:S(2)}) copy-start(bf16[32,256]{1,0:T(8,128)(2,1)S(1)} %collective-permute-done.11.refs_7_.refs_31_) | copy-start | bytes 49156
  138.5 11.6 %copy-start.43 = (bf16[1,8,4096]{2,1,0:T(8,128)(2,1)S(1)}, bf16[1,8,4096]{2,1,0:T(8,128)(2,1)}, u32[]{:S(2)}) copy-start(bf16[1,8,4096]{2,1,0:T(8,128)(2,1)} %param.20) | copy-start | bytes 196612
  141.9 4.4 %collective-permute-start.13 = (bf16[8,4096]{1,0:T(8,128)(2,1)S(1)}, bf16[8,4096]{1,0:T(8,128)(2,1)S(1)}, u32[]{:S(2)}, u32[]{:S(2)}) collective-permute-start(bf16[8,4096]{1,0:T(8,128)(2,1)S(1)} %get-tuple-element.84), channel_id=1, source_target_pairs={{0,8},{8,0},{16,24},{24,16},{1,9},{9,1},{17,25},{25,17},{2,10},{10... | collective-permute-start | bytes 196616 | tf_op jit(solution)/shard_map/ppermute | solution.py:714
  143.4 4.3 %collective-permute-start.14 = (bf16[8,4096]{1,0:T(8,128)(2,1)S(1)}, bf16[8,4096]{1,0:T(8,128)(2,1)S(1)}, u32[]{:S(2)}, u32[]{:S(2)}) collective-permute-start(bf16[8,4096]{1,0:T(8,128)(2,1)S(1)} %get-tuple-element.85), channel_id=1, source_target_pairs={{0,16},{8,24},{16,0},{24,8},{1,17},{9,25},{17,1},{25,9},{2,18},{10... | collective-permute-start | bytes 196616 | tf_op jit(solution)/shard_map/ppermute | solution.py:714
  144.9 5.2 %collective-permute-start.15 = (bf16[8,4096]{1,0:T(8,128)(2,1)S(1)}, bf16[8,4096]{1,0:T(8,128)(2,1)S(1)}, u32[]{:S(2)}, u32[]{:S(2)}) collective-permute-start(bf16[8,4096]{1,0:T(8,128)(2,1)S(1)} %get-tuple-element.86), channel_id=1, source_target_pairs={{0,24},{8,16},{16,8},{24,0},{1,25},{9,17},{17,9},{25,1},{2,26},{10... | collective-permute-start | bytes 196616 | tf_op jit(solution)/shard_map/ppermute | solution.py:714
  180.3 3.0 %collective-permute-start.16 = (bf16[4,4,272,128]{3,2,1,0:T(8,128)(2,1)}, bf16[4,4,272,128]{3,2,1,0:T(8,128)(2,1)S(1)}, u32[]{:S(2)}, u32[]{:S(2)}) collective-permute-start(bf16[4,4,272,128]{3,2,1,0:T(8,128)(2,1)} %get-tuple-element.103), channel_id=1, source_target_pairs={{0,1},{1,0},{2,3},{3,2},{4,5},{5,4},{6,7},{7,6},{8,9},{9,8},{10,11... | collective-permute-start | bytes 3342344 | tf_op jit(solution)/shard_map/ppermute | solution.py:714
  184.6 46.4 %copy-start.14 = (s32[6]{0:T(128)S(1)}, s32[6]{0:T(128)}, u32[]{:S(2)}) copy-start(s32[6]{0:T(128)} %copy-done.12) | copy-start | bytes 76
  184.8 9.6 %collective-permute-start.17 = (bf16[4,272,128]{2,1,0:T(8,128)(2,1)S(1)}, bf16[4,272,128]{2,1,0:T(8,128)(2,1)S(1)}, u32[]{:S(2)}, u32[]{:S(2)}) collective-permute-start(bf16[4,272,128]{2,1,0:T(8,128)(2,1)S(1)} %get-tuple-element.105), channel_id=1, source_target_pairs={{0,8},{8,0},{16,24},{24,16},{1,9},{9,1},{17,25},{25,17},{2,10},{10... | collective-permute-start | bytes 835592 | tf_op jit(solution)/shard_map/ppermute | solution.py:714
  185.4 14.4 %collective-permute-start.18 = (bf16[4,272,128]{2,1,0:T(8,128)(2,1)S(1)}, bf16[4,272,128]{2,1,0:T(8,128)(2,1)S(1)}, u32[]{:S(2)}, u32[]{:S(2)}) collective-permute-start(bf16[4,272,128]{2,1,0:T(8,128)(2,1)S(1)} %get-tuple-element.106), channel_id=1, source_target_pairs={{0,16},{8,24},{16,0},{24,8},{1,17},{9,25},{17,1},{25,9},{2,18},{10... | collective-permute-start | bytes 835592 | tf_op jit(solution)/shard_map/ppermute | solution.py:714
  186.0 13.8 %collective-permute-start.19 = (bf16[4,272,128]{2,1,0:T(8,128)(2,1)S(1)}, bf16[4,272,128]{2,1,0:T(8,128)(2,1)S(1)}, u32[]{:S(2)}, u32[]{:S(2)}) collective-permute-start(bf16[4,272,128]{2,1,0:T(8,128)(2,1)S(1)} %get-tuple-element.107), channel_id=1, source_target_pairs={{0,24},{8,16},{16,8},{24,0},{1,25},{9,17},{17,9},{25,1},{2,26},{10... | collective-permute-start | bytes 835592 | tf_op jit(solution)/shard_map/ppermute | solution.py:714
  200.0 4.8 %collective-permute-start.20 = (bf16[272,128]{1,0:T(8,128)(2,1)S(1)}, bf16[272,128]{1,0:T(8,128)(2,1)S(1)}, u32[]{:S(2)}, u32[]{:S(2)}) collective-permute-start(bf16[272,128]{1,0:T(8,128)(2,1)S(1)} %get-tuple-element.109), channel_id=1, source_target_pairs={{0,2},{1,3},{2,0},{3,1},{4,6},{5,7},{6,4},{7,5},{8,10},{9,11},{10,... | collective-permute-start | bytes 208904 | tf_op jit(solution)/shard_map/ppermute | solution.py:714
  201.0 7.5 %collective-permute-start.21 = (bf16[272,128]{1,0:T(8,128)(2,1)S(1)}, bf16[272,128]{1,0:T(8,128)(2,1)S(1)}, u32[]{:S(2)}, u32[]{:S(2)}) collective-permute-start(bf16[272,128]{1,0:T(8,128)(2,1)S(1)} %get-tuple-element.110), channel_id=1, source_target_pairs={{0,4},{1,5},{2,6},{3,7},{4,0},{5,1},{6,2},{7,3},{8,12},{9,13},{10,... | collective-permute-start | bytes 208904 | tf_op jit(solution)/shard_map/ppermute | solution.py:714
  201.8 6.7 %collective-permute-start.22 = (bf16[272,128]{1,0:T(8,128)(2,1)S(1)}, bf16[272,128]{1,0:T(8,128)(2,1)S(1)}, u32[]{:S(2)}, u32[]{:S(2)}) collective-permute-start(bf16[272,128]{1,0:T(8,128)(2,1)S(1)} %get-tuple-element.111), channel_id=1, source_target_pairs={{0,6},{1,7},{2,4},{3,5},{4,2},{5,3},{6,0},{7,1},{8,14},{9,15},{10,... | collective-permute-start | bytes 208904 | tf_op jit(solution)/shard_map/ppermute | solution.py:714
  208.5 6.3 %collective-permute-start.25 = (bf16[272,128]{1,0:T(8,128)(2,1)S(1)}, bf16[272,128]{1,0:T(8,128)(2,1)S(1)}, u32[]{:S(2)}, u32[]{:S(2)}) collective-permute-start(bf16[272,128]{1,0:T(8,128)(2,1)S(1)} %shard_map.245), channel_id=1, source_target_pairs={{0,6},{1,7},{2,4},{3,5},{4,2},{5,3},{6,0},{7,1},{8,14},{9,15},{10,... | collective-permute-start | bytes 208904 | tf_op jit(solution)/shard_map/ppermute | solution.py:714
  210.8 5.7 %collective-permute-start.24 = (bf16[272,128]{1,0:T(8,128)(2,1)S(1)}, bf16[272,128]{1,0:T(8,128)(2,1)S(1)}, u32[]{:S(2)}, u32[]{:S(2)}) collective-permute-start(bf16[272,128]{1,0:T(8,128)(2,1)S(1)} %shard_map.245), channel_id=1, source_target_pairs={{0,4},{1,5},{2,6},{3,7},{4,0},{5,1},{6,2},{7,3},{8,12},{9,13},{10,... | collective-permute-start | bytes 208904 | tf_op jit(solution)/shard_map/ppermute | solution.py:714
  211.3 5.1 %collective-permute-start.23 = (bf16[272,128]{1,0:T(8,128)(2,1)S(1)}, bf16[272,128]{1,0:T(8,128)(2,1)S(1)}, u32[]{:S(2)}, u32[]{:S(2)}) collective-permute-start(bf16[272,128]{1,0:T(8,128)(2,1)S(1)} %shard_map.245), channel_id=1, source_target_pairs={{0,2},{1,3},{2,0},{3,1},{4,6},{5,7},{6,4},{7,5},{8,10},{9,11},{10,... | collective-permute-start | bytes 208904 | tf_op jit(solution)/shard_map/ppermute | solution.py:714
  216.5 9.8 %collective-permute-start.28 = (bf16[4,272,128]{2,1,0:T(8,128)(2,1)S(1)}, bf16[4,272,128]{2,1,0:T(8,128)(2,1)S(1)}, u32[]{:S(2)}, u32[]{:S(2)}) collective-permute-start(bf16[4,272,128]{2,1,0:T(8,128)(2,1)S(1)} %pad_maximum_fusion.refs_0_), channel_id=1, source_target_pairs={{0,24},{8,16},{16,8},{24,0},{1,25},{9,17},{17,9},{25,1},{2,26},{10... | collective-permute-start | bytes 835592 | tf_op jit(solution)/shard_map/ppermute | solution.py:714
  218.0 11.0 %collective-permute-start.27 = (bf16[4,272,128]{2,1,0:T(8,128)(2,1)S(1)}, bf16[4,272,128]{2,1,0:T(8,128)(2,1)S(1)}, u32[]{:S(2)}, u32[]{:S(2)}) collective-permute-start(bf16[4,272,128]{2,1,0:T(8,128)(2,1)S(1)} %pad_maximum_fusion.refs_0_), channel_id=1, source_target_pairs={{0,16},{8,24},{16,0},{24,8},{1,17},{9,25},{17,1},{25,9},{2,18},{10... | collective-permute-start | bytes 835592 | tf_op jit(solution)/shard_map/ppermute | solution.py:714
  219.2 10.0 %collective-permute-start.26 = (bf16[4,272,128]{2,1,0:T(8,128)(2,1)S(1)}, bf16[4,272,128]{2,1,0:T(8,128)(2,1)S(1)}, u32[]{:S(2)}, u32[]{:S(2)}) collective-permute-start(bf16[4,272,128]{2,1,0:T(8,128)(2,1)S(1)} %pad_maximum_fusion.refs_0_), channel_id=1, source_target_pairs={{0,8},{8,0},{16,24},{24,16},{1,9},{9,1},{17,25},{25,17},{2,10},{10... | collective-permute-start | bytes 835592 | tf_op jit(solution)/shard_map/ppermute | solution.py:714
  220.0 10.2 %collective-permute-start.29 = (bf16[4,272,128]{2,1,0:T(8,128)(2,1)S(1)}, bf16[4,272,128]{2,1,0:T(8,128)(2,1)S(1)}, u32[]{:S(2)}, u32[]{:S(2)}) collective-permute-start(bf16[4,272,128]{2,1,0:T(8,128)(2,1)S(1)} %pad_maximum_fusion.refs_0_), channel_id=1, source_target_pairs={{0,1},{1,0},{2,3},{3,2},{4,5},{5,4},{6,7},{7,6},{8,9},{9,8},{10,11... | collective-permute-start | bytes 835592 | tf_op jit(solution)/shard_map/ppermute | solution.py:714
  226.2 4.0 %collective-permute-start.32 = (bf16[4,272,128]{2,1,0:T(8,128)(2,1)S(1)}, bf16[4,272,128]{2,1,0:T(8,128)(2,1)S(1)}, u32[]{:S(2)}, u32[]{:S(2)}) collective-permute-start(bf16[4,272,128]{2,1,0:T(8,128)(2,1)S(1)} %collective-permute-done.28.refs_3_), channel_id=1, source_target_pairs={{0,1},{1,0},{2,3},{3,2},{4,5},{5,4},{6,7},{7,6},{8,9},{9,8},{10,11... | collective-permute-start | bytes 835592 | tf_op jit(solution)/shard_map/ppermute | solution.py:714
  229.0 1.6 collective-permute-start.31
  229.2 1.8 collective-permute-start.30
  (32 other events, 50.2 us)
